TPU v7x, 128 devices: a whole 4x4x4 slice. The times are simulated.
128 devices in a mesh: rows: 8 (over y_lo, z), cols: 16 (over y_hi, x, core).
Axes of the slice: x: 4, y: 4 (y_hi: 2, y_lo: 2; y = y_hi * 2 + y_lo), z: 4, core: 2. Of those that a mesh axis runs over, the one named last changes fastest.
Arguments:
- features: bfloat16 [128, 1024, 180], P('rows', 'cols'), may hold values from -8 to 8
- gain_one: float32 [180], replicated, may hold values from 0.1 to 1.9
- qkv_weight: bfloat16 [180, 540], replicated, may hold values from -4 to 4
- bias_table: float32 [1521, 6], replicated, may hold values from -4 to 4
- proj_weight: bfloat16 [180, 180], replicated, may hold values from -0.4375 to 0.4375
- gain_two: float32 [180], replicated, may hold values from 0.1 to 1.9
- hidden_weight: bfloat16 [180, 360], replicated, may hold values from -0.4375 to 0.4375
- output_weight: bfloat16 [360, 180], replicated, may hold values from -0.3125 to 0.3125
- group_conv: bfloat16 [3, 3, 180, 180], replicated, may hold values from -0.15625 to 0.15625
- before_conv: bfloat16 [3, 3, 180, 64], replicated, may hold values from -0.15625 to 0.15625
- upsample_conv: bfloat16 [3, 3, 64, 256], replicated, may hold values from -0.25 to 0.25
Outputs:
- upscaled: bfloat16 [64, 256, 2048], P(None, 'rows', 'cols')
All inputs are finite; a program needn't handle non-finite values.
Results may differ from a plain program's by a relative error of at most 0.017.
Values may be sent and summed in bfloat16 or wider, within the bound.
A program may use at most 128 MiB of HBM per device.

v0:
```python
import jax
import jax.numpy as jnp
import numpy as np
from jax import lax
from jax.sharding import PartitionSpec as P

HEADS = 6
WIN = 16
KWIN = 24


def padded_2(block, sides, width):
    for axis, dim in sides:
        count = lax.axis_size(axis)
        forward = [(i, i + 1) for i in range(count - 1)]
        backward = [(target, source) for source, target in forward]
        low = lax.ppermute(
            lax.slice_in_dim(block, block.shape[dim] - width, None, axis=dim), axis, forward
        )
        high = lax.ppermute(lax.slice_in_dim(block, 0, width, axis=dim), axis, backward)
        block = jnp.concatenate([low, block, high], axis=dim)
    return block


def layer_norm(values, gain):
    center = values - jnp.mean(values, axis=-1, keepdims=True)
    spread = jnp.mean(center * center, axis=-1, keepdims=True)
    return center * lax.rsqrt(spread + 1e-05) * gain


def offset_selector():
    side = WIN + KWIN - 1
    query_pos = np.arange(WIN)[:, None, None]
    key_pos = np.arange(KWIN)[None, :, None]
    entry = np.arange(side)[None, None, :]
    return (entry == key_pos - query_pos + WIN - 1).astype(np.float32)


def build_bias(bias_table):
    side = WIN + KWIN - 1
    grid = bias_table.reshape(side, side, HEADS)
    selector = jnp.asarray(offset_selector())
    partial_rows = jnp.einsum("ipa,abh->hipb", selector, grid, precision=lax.Precision.HIGHEST)
    full = jnp.einsum("jqb,hipb->hijpq", selector, partial_rows, precision=lax.Precision.HIGHEST)
    return full.reshape(HEADS, WIN * WIN, KWIN * KWIN)


def query_windows(values):
    height, width, chans = values.shape
    blocks = values.reshape(height // WIN, WIN, width // WIN, WIN, chans)
    return blocks.transpose(0, 2, 1, 3, 4).reshape(-1, WIN * WIN, chans)


def undo_windows(values, height, width):
    chans = values.shape[-1]
    blocks = values.reshape(height // WIN, width // WIN, WIN, WIN, chans)
    return blocks.transpose(0, 2, 1, 3, 4).reshape(height, width, chans)


def key_windows(padded):
    span = KWIN - WIN
    height, width, chans = padded.shape
    nbr = height // span
    nbc = width // span
    blocks = padded.reshape(nbr, span, nbc, span, chans)
    stacked = jnp.stack([blocks[0 : nbr - 1 : 2], blocks[1:nbr:2], blocks[2:nbr:2]], axis=1)
    stacked = jnp.stack(
        [stacked[:, :, :, 0 : nbc - 1 : 2], stacked[:, :, :, 1:nbc:2], stacked[:, :, :, 2:nbc:2]],
        axis=4,
    )
    stacked = stacked.transpose(0, 3, 1, 2, 4, 5, 6)
    return stacked.reshape(-1, KWIN * KWIN, chans)


def attend_group(query_block, keyval_block, bias):
    groups = query_block.shape[0]
    chans = query_block.shape[-1]
    head_size = chans // HEADS
    qs = query_block.reshape(groups, WIN * WIN, HEADS, head_size)
    keys = keyval_block[..., :chans].reshape(groups, KWIN * KWIN, HEADS, head_size)
    vals = keyval_block[..., chans:].reshape(groups, KWIN * KWIN, HEADS, head_size)
    scores = (
        jnp.einsum("gqhd,gkhd->ghqk", qs, keys, preferred_element_type=jnp.float32)
        / jnp.sqrt(jnp.float32(head_size))
        + bias[None]
    )
    probs = jax.nn.softmax(scores, axis=-1).astype(jnp.bfloat16)
    result = jnp.einsum("ghqk,gkhd->gqhd", probs, vals, preferred_element_type=jnp.float32)
    return result.reshape(groups, WIN * WIN, chans).astype(jnp.bfloat16)


def conv_last(padded, weight):
    height = padded.shape[0] - 2
    width = padded.shape[1] - 2
    total = jnp.zeros((height, width, weight.shape[3]), jnp.float32)
    for tap_r in range(3):
        for tap_c in range(3):
            total = total + jnp.dot(
                padded[tap_r : tap_r + height, tap_c : tap_c + width],
                weight[tap_r, tap_c],
                preferred_element_type=jnp.float32,
            )
    return total


def conv_to_first(padded, weight):
    height = padded.shape[0] - 2
    width = padded.shape[1] - 2
    total = jnp.zeros((weight.shape[3], height, width), jnp.float32)
    for tap_r in range(3):
        for tap_c in range(3):
            total = total + jnp.einsum(
                "hwc,co->ohw",
                padded[tap_r : tap_r + height, tap_c : tap_c + width],
                weight[tap_r, tap_c],
                preferred_element_type=jnp.float32,
            )
    return total


def conv_first(padded, weight):
    height = padded.shape[1] - 2
    width = padded.shape[2] - 2
    total = jnp.zeros((weight.shape[3], height, width), jnp.float32)
    for tap_r in range(3):
        for tap_c in range(3):
            total = total + jnp.einsum(
                "chw,co->ohw",
                padded[:, tap_r : tap_r + height, tap_c : tap_c + width],
                weight[tap_r, tap_c],
                preferred_element_type=jnp.float32,
            )
    return total


def shuffle(expanded):
    chans4, height, width = expanded.shape
    chans = chans4 // 4
    parts = expanded.reshape(chans, 2, 2, height, width).transpose(0, 3, 1, 4, 2)
    return parts.reshape(chans, 2 * height, 2 * width)


def on_device(
    features,
    gain_one,
    qkv_weight,
    bias_table,
    proj_weight,
    gain_two,
    hidden_weight,
    output_weight,
    group_conv,
    before_conv,
    upsample_conv,
):
    height, width, chans = features.shape
    rim = (KWIN - WIN) // 2
    base = features.astype(jnp.float32)
    normed = layer_norm(base, gain_one).astype(jnp.bfloat16)
    projected = jnp.dot(normed, qkv_weight, preferred_element_type=jnp.float32)
    queries = projected[..., :chans].astype(jnp.bfloat16)
    keyvals = projected[..., chans:].astype(jnp.bfloat16)
    padded = padded_2(keyvals, (("rows", 0), ("cols", 1)), rim)
    bias = build_bias(bias_table)
    query_win = query_windows(queries)
    keyval_win = key_windows(padded)
    count = query_win.shape[0]
    group = 4
    attended = lax.map(
        lambda pair: attend_group(pair[0], pair[1], bias),
        (
            query_win.reshape(count // group, group, WIN * WIN, chans),
            keyval_win.reshape(count // group, group, KWIN * KWIN, 2 * chans),
        ),
    )
    attended = undo_windows(attended.reshape(count, WIN * WIN, chans), height, width)
    first = base + jnp.dot(attended, proj_weight, preferred_element_type=jnp.float32)
    second_norm = layer_norm(first, gain_two).astype(jnp.bfloat16)
    inner = jax.nn.gelu(
        jnp.dot(second_norm, hidden_weight, preferred_element_type=jnp.float32), approximate=False
    ).astype(jnp.bfloat16)
    mixed = (first + jnp.dot(inner, output_weight, preferred_element_type=jnp.float32)).astype(
        jnp.bfloat16
    )
    mixed_pad = padded_2(mixed, (("rows", 0), ("cols", 1)), 1)
    grouped = (base + conv_last(mixed_pad, group_conv)).astype(jnp.bfloat16)
    grouped_pad = padded_2(grouped, (("rows", 0), ("cols", 1)), 1)
    lowfeat = jax.nn.leaky_relu(conv_to_first(grouped_pad, before_conv), 0.01).astype(jnp.bfloat16)
    lowfeat_pad = padded_2(lowfeat, (("rows", 1), ("cols", 2)), 1)
    expanded = conv_first(lowfeat_pad, upsample_conv)
    return shuffle(expanded).astype(jnp.bfloat16)


def solution(mesh):
    placed = (P("rows", "cols", None), P(), P(), P(), P(), P(), P(), P(), P(), P(), P())
    return jax.shard_map(
        on_device, mesh=mesh, in_specs=placed, out_specs=P(None, "rows", "cols"), check_vma=False
    )
```

profile of v0, /device:TPU:103, one launch (start us, length us, event | category | flops | bytes accessed | tf_op | source)
XLA Modules:
  0.0 192.7 jit_solution(496283286797525040)
XLA Ops:
  6.7 3.4 %collective-permute-start.1 = (bf16[4,64,360]{2,1,0:T(8,128)(2,1)S(1)}, bf16[4,64,360]{2,1,0:T(8,128)(2,1)S(1)}, u32[]{:S(2)}, u32[]{:S(2)}) collective-permute-start(bf16[4,64,360]{2,1,0:T(8,128)(2,1)S(1)} %get-tuple-element.31), channel_id=1, source_target_pairs={{16,0},{32,16},{48,32},{64,48},{80,64},{96,80},{112,96},{17,1},{33... | collective-permute-start | bytes 552968 | tf_op jit(solution)/shard_map/ppermute | solution.py:20
  12.5 3.8 %collective-permute-done.1 = bf16[4,64,360]{2,1,0:T(8,128)(2,1)S(1)} collective-permute-done((bf16[4,64,360]{2,1,0:T(8,128)(2,1)S(1)}, bf16[4,64,360]{2,1,0:T(8,128)(2,1)S(1)}, u32[]{:S(2)}, u32[]{:S(2)}) %collective-permute-start.1) | collective-permute-done | bytes 184352 | tf_op jit(solution)/shard_map/ppermute | solution.py:20
  16.4 6.4 %collective-permute-start.2 = (bf16[24,4,360]{2,1,0:T(4,128)(2,1)S(1)}, bf16[24,4,360]{2,1,0:T(4,128)(2,1)S(1)}, u32[]{:S(2)}, u32[]{:S(2)}) collective-permute-start(bf16[24,4,360]{2,1,0:T(4,128)(2,1)S(1)} %get-tuple-element.32), channel_id=1, source_target_pairs={{0,1},{1,2},{2,3},{3,4},{4,5},{5,6},{6,7},{7,8},{8,9},{9,10},{10,1... | collective-permute-start | bytes 207368 | tf_op jit(solution)/shard_map/ppermute | solution.py:17
  24.9 18.2 %convolution_bitcast_fusion = f32[6,16,16,24,24]{4,3,2,1,0:T(8,128)} fusion(f32[6,16,24,39,1]{3,2,4,1,0:T(8,128)S(1)} %convolution_bitcast_fusion.1, f32[16,24,39,1,1]{2,1,0,4,3:T(8,128)S(1)} %copy-done.7), kind=kOutput, calls=%fused_computation.5 | convolution fusion | flops 414056448 | bytes 3958272 | tf_op jit(solution)/shard_map/jqb,hipb->hijpq/dot_general | solution.py:44
  44.0 2.7 %reshape.80 = bf16[4,256,6,30]{3,2,1,0:T(8,128)(2,1)S(1)} reshape(bf16[1,4,16,16,180]{4,3,2,1,0:T(8,128)(2,1)} %bitcast.226) | data formatting | bytes 737280 | tf_op jit(solution)/shard_map/while/body/eval_jaxpr/reshape | solution.py:79
  46.7 13.5 %add.126 = f32[6,256,576]{2,1,0:T(8,128)} reshape(f32[6,16,16,24,24]{4,3,2,1,0:T(8,128)} %convolution_bitcast_fusion) | data formatting | bytes 7077888 | tf_op jit(solution)/shard_map/while/body/eval_jaxpr/add | solution.py:83
  60.1 5.3 %copy.43 = f32[6,256,576]{1,2,0:T(8,128)} copy(f32[6,256,576]{2,1,0:T(8,128)} %add.126) | data formatting | bytes 7077888 | tf_op jit(solution)/shard_map/while/body/eval_jaxpr/add | solution.py:83
  72.0 2.7 %copy.40 = bf16[4,576,180]{1,0,2:T(4,128)(2,1)S(1)} copy(bf16[4,576,180]{2,1,0:T(8,128)(2,1)} %get-tuple-element.22) | data formatting | bytes 1658880 | tf_op jit(solution)/shard_map/while/body/eval_jaxpr/slice | solution.py:80
  74.7 7.1 %fusion.8 = f32[4,6,256,576]{2,3,1,0:T(8,128)} fusion(bf16[4,256,6,30]{3,2,1,0:T(8,128)(2,1)S(1)} %reshape.80, bf16[4,576,6,30]{1,0,3,2:T(4,128)(2,1)S(1)} %bitcast.222), kind=kOutput, calls=%fused_computation.24 | convolution fusion | flops 212336640 | bytes 15353856 | tf_op jit(solution)/shard_map/while/body/eval_jaxpr/gqhd,gkhd->ghqk/dot_general | solution.py:83
  81.8 19.1 %fusion.253 = (f32[4,6,256]{2,1,0:T(8,128)S(1)}, f32[4,6,256,576]{2,3,1,0:T(8,128)}) fusion(f32[4,6,256,576]{2,3,1,0:T(8,128)} %fusion.8, f32[6,256,576]{1,2,0:T(8,128)} %copy.43), kind=kOutput, calls=%fused_computation.316 | output fusion | flops 21234240 | bytes 31875072 | tf_op jit(solution)/shard_map/while/body/eval_jaxpr/sub | solution.py:87
  100.9 6.3 %fusion.42 = bf16[4,256,6,30]{1,3,2,0:T(8,128)(2,1)S(1)} fusion(f32[4,6,256,576]{2,3,1,0:T(8,128)} %get-tuple-element.53, f32[4,6,256]{2,1,0:T(8,128)S(1)} %get-tuple-element.52, bf16[4,576,6,30]{1,0,3,2:T(4,128)(2,1)S(1)} %bitcast.230), kind=kOutput, calls=%fused_computation.76 | convolution fusion | flops 219598848 | bytes 15378432 | tf_op jit(solution)/shard_map/while/body/eval_jaxpr/ghqk,gkhd->gqhd/dot_general | solution.py:88
  111.6 3.8 %fusion.28 = bf16[16,64,180]{2,1,0:T(8,128)(2,1)S(1)} fusion(f32[16,64,180]{2,1,0:T(8,128)S(1)} %get-tuple-element.55, f32[16,64,360]{2,1,0:T(8,128)S(1)} %get-tuple-element.56, u16[64,360]{1,0:T(8,128)(2,1)S(1)} %get-tuple-element.14, u16[64,360]{1,0:T(8,128)(2,1)S(1)} %get-tuple-element.13, bf16[360,180]{0,1:T(8,128)(2,1)S(1)} %copy-done.12), kind=kOutput, calls=%fused_computation.60 | convolution fusion | flops 158883840 | bytes 2802240 | tf_op jit(solution)/shard_map/dot_general | solution.py:182
  117.4 3.4 %collective-permute-start.5 = (bf16[1,64,180]{2,1,0:T(8,128)(2,1)S(1)}, bf16[1,64,180]{2,1,0:T(8,128)(2,1)S(1)}, u32[]{:S(2)}, u32[]{:S(2)}) collective-permute-start(bf16[1,64,180]{2,1,0:T(8,128)(2,1)S(1)} %get-tuple-element.45), channel_id=1, source_target_pairs={{16,0},{32,16},{48,32},{64,48},{80,64},{96,80},{112,96},{17,1},{33... | collective-permute-start | bytes 69128 | tf_op jit(solution)/shard_map/ppermute | solution.py:20
  121.1 3.1 %collective-permute-done.5 = bf16[1,64,180]{2,1,0:T(8,128)(2,1)S(1)} collective-permute-done((bf16[1,64,180]{2,1,0:T(8,128)(2,1)S(1)}, bf16[1,64,180]{2,1,0:T(8,128)(2,1)S(1)}, u32[]{:S(2)}, u32[]{:S(2)}) %collective-permute-start.5) | collective-permute-done | bytes 23072 | tf_op jit(solution)/shard_map/ppermute | solution.py:20
  124.2 8.4 %collective-permute-start.6 = (bf16[18,1,180]{2,1,0:T(2,128)(2,1)S(1)}, bf16[18,1,180]{2,1,0:T(2,128)(2,1)S(1)}, u32[]{:S(2)}, u32[]{:S(2)}) collective-permute-start(bf16[18,1,180]{2,1,0:T(2,128)(2,1)S(1)} %get-tuple-element.40), channel_id=1, source_target_pairs={{0,1},{1,2},{2,3},{3,4},{4,5},{5,6},{6,7},{7,8},{8,9},{9,10},{10,1... | collective-permute-start | bytes 19448 | tf_op jit(solution)/shard_map/ppermute | solution.py:17
  135.2 6.2 %collective-permute-done.7 = bf16[18,1,180]{2,1,0:T(2,128)(2,1)S(1)} collective-permute-done((bf16[18,1,180]{2,1,0:T(2,128)(2,1)S(1)}, bf16[18,1,180]{2,1,0:T(2,128)(2,1)S(1)}, u32[]{:S(2)}, u32[]{:S(2)}) %collective-permute-start.7) | collective-permute-done | bytes 6512 | tf_op jit(solution)/shard_map/ppermute | solution.py:20
  145.6 3.4 %collective-permute-start.9 = (bf16[1,64,180]{2,1,0:T(8,128)(2,1)S(1)}, bf16[1,64,180]{2,1,0:T(8,128)(2,1)S(1)}, u32[]{:S(2)}, u32[]{:S(2)}) collective-permute-start(bf16[1,64,180]{2,1,0:T(8,128)(2,1)S(1)} %get-tuple-element.43), channel_id=1, source_target_pairs={{16,0},{32,16},{48,32},{64,48},{80,64},{96,80},{112,96},{17,1},{33... | collective-permute-start | bytes 69128 | tf_op jit(solution)/shard_map/ppermute | solution.py:20
  149.3 3.1 %collective-permute-done.9 = bf16[1,64,180]{2,1,0:T(8,128)(2,1)S(1)} collective-permute-done((bf16[1,64,180]{2,1,0:T(8,128)(2,1)S(1)}, bf16[1,64,180]{2,1,0:T(8,128)(2,1)S(1)}, u32[]{:S(2)}, u32[]{:S(2)}) %collective-permute-start.9) | collective-permute-done | bytes 23072 | tf_op jit(solution)/shard_map/ppermute | solution.py:20
  152.4 3.1 %collective-permute-start.10 = (bf16[18,1,180]{2,1,0:T(2,128)(2,1)S(1)}, bf16[18,1,180]{2,1,0:T(2,128)(2,1)S(1)}, u32[]{:S(2)}, u32[]{:S(2)}) collective-permute-start(bf16[18,1,180]{2,1,0:T(2,128)(2,1)S(1)} %get-tuple-element.36), channel_id=1, source_target_pairs={{0,1},{1,2},{2,3},{3,4},{4,5},{5,6},{6,7},{7,8},{8,9},{9,10},{10,1... | collective-permute-start | bytes 19448 | tf_op jit(solution)/shard_map/ppermute | solution.py:17
  158.3 5.9 %collective-permute-done.11 = bf16[18,1,180]{2,1,0:T(2,128)(2,1)S(1)} collective-permute-done((bf16[18,1,180]{2,1,0:T(2,128)(2,1)S(1)}, bf16[18,1,180]{2,1,0:T(2,128)(2,1)S(1)}, u32[]{:S(2)}, u32[]{:S(2)}) %collective-permute-start.11) | collective-permute-done | bytes 6512 | tf_op jit(solution)/shard_map/ppermute | solution.py:20
  168.3 3.4 %collective-permute-start.13 = (bf16[64,1,64]{0,2,1:T(8,128)(2,1)S(1)}, bf16[64,1,64]{0,2,1:T(8,128)(2,1)S(1)}, u32[]{:S(2)}, u32[]{:S(2)}) collective-permute-start(bf16[64,1,64]{0,2,1:T(8,128)(2,1)S(1)} %get-tuple-element.51), channel_id=1, source_target_pairs={{16,0},{32,16},{48,32},{64,48},{80,64},{96,80},{112,96},{17,1},{33... | collective-permute-start | bytes 24584 | tf_op jit(solution)/shard_map/ppermute | solution.py:20
  172.0 2.9 %collective-permute-done.13 = bf16[64,1,64]{0,2,1:T(8,128)(2,1)S(1)} collective-permute-done((bf16[64,1,64]{0,2,1:T(8,128)(2,1)S(1)}, bf16[64,1,64]{0,2,1:T(8,128)(2,1)S(1)}, u32[]{:S(2)}, u32[]{:S(2)}) %collective-permute-start.13) | collective-permute-done | bytes 8224 | tf_op jit(solution)/shard_map/ppermute | solution.py:20
  175.0 3.1 %collective-permute-start.14 = (bf16[64,18,1]{0,2,1:T(2,128)(2,1)S(1)}, bf16[64,18,1]{0,2,1:T(2,128)(2,1)S(1)}, u32[]{:S(2)}, u32[]{:S(2)}) collective-permute-start(bf16[64,18,1]{0,2,1:T(2,128)(2,1)S(1)} %get-tuple-element.48), channel_id=1, source_target_pairs={{0,1},{1,2},{2,3},{3,4},{4,5},{5,6},{6,7},{7,8},{8,9},{9,10},{10,1... | collective-permute-start | bytes 6920 | tf_op jit(solution)/shard_map/ppermute | solution.py:17
  180.5 6.1 %collective-permute-done.15 = bf16[64,18,1]{0,2,1:T(2,128)(2,1)S(1)} collective-permute-done((bf16[64,18,1]{0,2,1:T(2,128)(2,1)S(1)}, bf16[64,18,1]{0,2,1:T(2,128)(2,1)S(1)}, u32[]{:S(2)}, u32[]{:S(2)}) %collective-permute-start.15) | collective-permute-done | bytes 2336 | tf_op jit(solution)/shard_map/ppermute | solution.py:20
  (113 shorter events, 47.7 us)
Async XLA Ops:
  4.6 5.9 %copy-start.10 = (f32[1521,6]{0,1:T(8,128)S(1)}, f32[1521,6]{0,1:T(8,128)}, u32[]{:S(2)}) copy-start(f32[1521,6]{0,1:T(8,128)} %param.15) | copy-start | bytes 109516
  4.6 6.0 %copy-start.8 = (f32[16,24,39,1]{2,1,0,3:T(8,128)S(1)}, f32[16,24,39,1]{2,1,0,3:T(8,128)}, u32[]{:S(2)}) copy-start(f32[16,24,39,1]{2,1,0,3:T(8,128)} %constant.98) | copy-start | bytes 179716
  4.8 7.7 %collective-permute-start = (bf16[4,64,360]{2,1,0:T(8,128)(2,1)S(1)}, bf16[4,64,360]{2,1,0:T(8,128)(2,1)S(1)}, u32[]{:S(2)}, u32[]{:S(2)}) collective-permute-start(bf16[4,64,360]{2,1,0:T(8,128)(2,1)S(1)} %get-tuple-element.30), channel_id=1, source_target_pairs={{0,16},{16,32},{32,48},{48,64},{64,80},{80,96},{96,112},{1,17},{17... | collective-permute-start | bytes 552968 | tf_op jit(solution)/shard_map/ppermute | solution.py:17
  6.7 9.5 %collective-permute-start.1 = (bf16[4,64,360]{2,1,0:T(8,128)(2,1)S(1)}, bf16[4,64,360]{2,1,0:T(8,128)(2,1)S(1)}, u32[]{:S(2)}, u32[]{:S(2)}) collective-permute-start(bf16[4,64,360]{2,1,0:T(8,128)(2,1)S(1)} %get-tuple-element.31), channel_id=1, source_target_pairs={{16,0},{32,16},{48,32},{64,48},{80,64},{96,80},{112,96},{17,1},{33... | collective-permute-start | bytes 552968 | tf_op jit(solution)/shard_map/ppermute | solution.py:20
  10.5 14.4 %copy-start.7 = (f32[16,24,39,1,1]{2,1,0,4,3:T(8,128)S(1)}, f32[16,24,39,1,1]{2,1,0,4,3:T(8,128)}, u32[]{:S(2)}) copy-start(f32[16,24,39,1,1]{2,1,0,4,3:T(8,128)} %constant.99) | copy-start | bytes 179716
  16.4 49.1 %collective-permute-start.2 = (bf16[24,4,360]{2,1,0:T(4,128)(2,1)S(1)}, bf16[24,4,360]{2,1,0:T(4,128)(2,1)S(1)}, u32[]{:S(2)}, u32[]{:S(2)}) collective-permute-start(bf16[24,4,360]{2,1,0:T(4,128)(2,1)S(1)} %get-tuple-element.32), channel_id=1, source_target_pairs={{0,1},{1,2},{2,3},{3,4},{4,5},{5,6},{6,7},{7,8},{8,9},{9,10},{10,1... | collective-permute-start | bytes 207368 | tf_op jit(solution)/shard_map/ppermute | solution.py:17
  22.8 42.7 %collective-permute-start.3 = (bf16[24,4,360]{2,1,0:T(4,128)(2,1)S(1)}, bf16[24,4,360]{2,1,0:T(4,128)(2,1)}, u32[]{:S(2)}, u32[]{:S(2)}) collective-permute-start(bf16[24,4,360]{2,1,0:T(4,128)(2,1)S(1)} %get-tuple-element.33), channel_id=1, source_target_pairs={{1,0},{2,1},{3,2},{4,3},{5,4},{6,5},{7,6},{8,7},{9,8},{10,9},{11,1... | collective-permute-start | bytes 207368 | tf_op jit(solution)/shard_map/ppermute | solution.py:20
  81.8 19.1 %copy-start.3 = (bf16[4,576,180]{1,0,2:T(4,128)(2,1)S(1)}, bf16[4,576,180]{1,0,2:T(4,128)(2,1)}, u32[]{:S(2)}) copy-start(bf16[4,576,180]{1,0,2:T(4,128)(2,1)} %copy.38) | copy-start | bytes 2488324
  111.6 9.2 %copy-start.4 = (bf16[3,3,180,180]{3,2,1,0:T(8,128)(2,1)S(1)}, bf16[3,3,180,180]{3,2,1,0:T(8,128)(2,1)}, u32[]{:S(2)}) copy-start(bf16[3,3,180,180]{3,2,1,0:T(8,128)(2,1)} %param.20) | copy-start | bytes 1749604
  115.5 5.6 %collective-permute-start.4 = (bf16[1,64,180]{2,1,0:T(8,128)(2,1)S(1)}, bf16[1,64,180]{2,1,0:T(8,128)(2,1)S(1)}, u32[]{:S(2)}, u32[]{:S(2)}) collective-permute-start(bf16[1,64,180]{2,1,0:T(8,128)(2,1)S(1)} %get-tuple-element.44), channel_id=1, source_target_pairs={{0,16},{16,32},{32,48},{48,64},{64,80},{80,96},{96,112},{1,17},{17... | collective-permute-start | bytes 69128 | tf_op jit(solution)/shard_map/ppermute | solution.py:17
  117.4 6.8 %collective-permute-start.5 = (bf16[1,64,180]{2,1,0:T(8,128)(2,1)S(1)}, bf16[1,64,180]{2,1,0:T(8,128)(2,1)S(1)}, u32[]{:S(2)}, u32[]{:S(2)}) collective-permute-start(bf16[1,64,180]{2,1,0:T(8,128)(2,1)S(1)} %get-tuple-element.45), channel_id=1, source_target_pairs={{16,0},{32,16},{48,32},{64,48},{80,64},{96,80},{112,96},{17,1},{33... | collective-permute-start | bytes 69128 | tf_op jit(solution)/shard_map/ppermute | solution.py:20
  124.2 11.0 %collective-permute-start.6 = (bf16[18,1,180]{2,1,0:T(2,128)(2,1)S(1)}, bf16[18,1,180]{2,1,0:T(2,128)(2,1)S(1)}, u32[]{:S(2)}, u32[]{:S(2)}) collective-permute-start(bf16[18,1,180]{2,1,0:T(2,128)(2,1)S(1)} %get-tuple-element.40), channel_id=1, source_target_pairs={{0,1},{1,2},{2,3},{3,4},{4,5},{5,6},{6,7},{7,8},{8,9},{9,10},{10,1... | collective-permute-start | bytes 19448 | tf_op jit(solution)/shard_map/ppermute | solution.py:17
  132.7 8.7 %collective-permute-start.7 = (bf16[18,1,180]{2,1,0:T(2,128)(2,1)S(1)}, bf16[18,1,180]{2,1,0:T(2,128)(2,1)S(1)}, u32[]{:S(2)}, u32[]{:S(2)}) collective-permute-start(bf16[18,1,180]{2,1,0:T(2,128)(2,1)S(1)} %get-tuple-element.41), channel_id=1, source_target_pairs={{1,0},{2,1},{3,2},{4,3},{5,4},{6,5},{7,6},{8,7},{9,8},{10,9},{11,1... | collective-permute-start | bytes 19448 | tf_op jit(solution)/shard_map/ppermute | solution.py:20
  143.2 5.8 %copy-start.5 = (bf16[3,3,180,64]{2,3,1,0:T(8,128)(2,1)S(1)}, bf16[3,3,180,64]{2,3,1,0:T(8,128)(2,1)}, u32[]{:S(2)}) copy-start(bf16[3,3,180,64]{2,3,1,0:T(8,128)(2,1)} %param.21) | copy-start | bytes 622084
  143.7 5.6 %collective-permute-start.8 = (bf16[1,64,180]{2,1,0:T(8,128)(2,1)S(1)}, bf16[1,64,180]{2,1,0:T(8,128)(2,1)S(1)}, u32[]{:S(2)}, u32[]{:S(2)}) collective-permute-start(bf16[1,64,180]{2,1,0:T(8,128)(2,1)S(1)} %get-tuple-element.42), channel_id=1, source_target_pairs={{0,16},{16,32},{32,48},{48,64},{64,80},{80,96},{96,112},{1,17},{17... | collective-permute-start | bytes 69128 | tf_op jit(solution)/shard_map/ppermute | solution.py:17
  145.6 6.8 %collective-permute-start.9 = (bf16[1,64,180]{2,1,0:T(8,128)(2,1)S(1)}, bf16[1,64,180]{2,1,0:T(8,128)(2,1)S(1)}, u32[]{:S(2)}, u32[]{:S(2)}) collective-permute-start(bf16[1,64,180]{2,1,0:T(8,128)(2,1)S(1)} %get-tuple-element.43), channel_id=1, source_target_pairs={{16,0},{32,16},{48,32},{64,48},{80,64},{96,80},{112,96},{17,1},{33... | collective-permute-start | bytes 69128 | tf_op jit(solution)/shard_map/ppermute | solution.py:20
  152.4 5.9 %collective-permute-start.10 = (bf16[18,1,180]{2,1,0:T(2,128)(2,1)S(1)}, bf16[18,1,180]{2,1,0:T(2,128)(2,1)S(1)}, u32[]{:S(2)}, u32[]{:S(2)}) collective-permute-start(bf16[18,1,180]{2,1,0:T(2,128)(2,1)S(1)} %get-tuple-element.36), channel_id=1, source_target_pairs={{0,1},{1,2},{2,3},{3,4},{4,5},{5,6},{6,7},{7,8},{8,9},{9,10},{10,1... | collective-permute-start | bytes 19448 | tf_op jit(solution)/shard_map/ppermute | solution.py:17
  155.5 8.7 %collective-permute-start.11 = (bf16[18,1,180]{2,1,0:T(2,128)(2,1)S(1)}, bf16[18,1,180]{2,1,0:T(2,128)(2,1)S(1)}, u32[]{:S(2)}, u32[]{:S(2)}) collective-permute-start(bf16[18,1,180]{2,1,0:T(2,128)(2,1)S(1)} %get-tuple-element.37), channel_id=1, source_target_pairs={{1,0},{2,1},{3,2},{4,3},{5,4},{6,5},{7,6},{8,7},{9,8},{10,9},{11,1... | collective-permute-start | bytes 19448 | tf_op jit(solution)/shard_map/ppermute | solution.py:20
  166.0 5.7 %copy-start.6 = (bf16[3,3,64,256]{3,2,1,0:T(8,128)(2,1)S(1)}, bf16[3,3,64,256]{3,2,1,0:T(8,128)(2,1)}, u32[]{:S(2)}) copy-start(bf16[3,3,64,256]{3,2,1,0:T(8,128)(2,1)} %param.22) | copy-start | bytes 884740
  166.4 5.6 %collective-permute-start.12 = (bf16[64,1,64]{0,2,1:T(8,128)(2,1)S(1)}, bf16[64,1,64]{0,2,1:T(8,128)(2,1)S(1)}, u32[]{:S(2)}, u32[]{:S(2)}) collective-permute-start(bf16[64,1,64]{0,2,1:T(8,128)(2,1)S(1)} %get-tuple-element.50), channel_id=1, source_target_pairs={{0,16},{16,32},{32,48},{48,64},{64,80},{80,96},{96,112},{1,17},{17... | collective-permute-start | bytes 24584 | tf_op jit(solution)/shard_map/ppermute | solution.py:17
  168.3 6.6 %collective-permute-start.13 = (bf16[64,1,64]{0,2,1:T(8,128)(2,1)S(1)}, bf16[64,1,64]{0,2,1:T(8,128)(2,1)S(1)}, u32[]{:S(2)}, u32[]{:S(2)}) collective-permute-start(bf16[64,1,64]{0,2,1:T(8,128)(2,1)S(1)} %get-tuple-element.51), channel_id=1, source_target_pairs={{16,0},{32,16},{48,32},{64,48},{80,64},{96,80},{112,96},{17,1},{33... | collective-permute-start | bytes 24584 | tf_op jit(solution)/shard_map/ppermute | solution.py:20
  175.0 5.6 %collective-permute-start.14 = (bf16[64,18,1]{0,2,1:T(2,128)(2,1)S(1)}, bf16[64,18,1]{0,2,1:T(2,128)(2,1)S(1)}, u32[]{:S(2)}, u32[]{:S(2)}) collective-permute-start(bf16[64,18,1]{0,2,1:T(2,128)(2,1)S(1)} %get-tuple-element.48), channel_id=1, source_target_pairs={{0,1},{1,2},{2,3},{3,4},{4,5},{5,6},{6,7},{7,8},{8,9},{9,10},{10,1... | collective-permute-start | bytes 6920 | tf_op jit(solution)/shard_map/ppermute | solution.py:17
  178.0 8.6 %collective-permute-start.15 = (bf16[64,18,1]{0,2,1:T(2,128)(2,1)S(1)}, bf16[64,18,1]{0,2,1:T(2,128)(2,1)S(1)}, u32[]{:S(2)}, u32[]{:S(2)}) collective-permute-start(bf16[64,18,1]{0,2,1:T(2,128)(2,1)S(1)} %get-tuple-element.49), channel_id=1, source_target_pairs={{1,0},{2,1},{3,2},{4,3},{5,4},{6,5},{7,6},{8,7},{9,8},{10,9},{11,1... | collective-permute-start | bytes 6920 | tf_op jit(solution)/shard_map/ppermute | solution.py:20
  189.6 3.1 %copy-start.1 = (bf16[180,540]{1,0:T(8,128)(2,1)S(1)}, bf16[180,540]{1,0:T(8,128)(2,1)}, u32[]{:S(2)}) copy-start(bf16[180,540]{1,0:T(8,128)(2,1)} %param.14) | copy-start | bytes 583204
  (6 other events, 8.0 us)
where the time goes:
time: 194 us; the launch traced here: 193 us
  starting transfers between devices  50.2 us (26%)
  matrix products  47.9 us (25%)
  local copies, waits for them, and re-layouts  36.6 us (19%)
  waiting for transfers between devices  31.9 us (16%)
  other arithmetic  25.4 us (13%)
    ppermute x8, waiting for transfers between devices, padded_2(): lax.ppermute(lax.slice_in_dim(block, 0, width, axis=dim), axis, backward)  31.1 us
    ppermute x8, starting transfers between devices, padded_2(): lax.ppermute(lax.slice_in_dim(block, block.shape[dim] - width, None, axis...  28.7 us
    ppermute x8, starting transfers between devices, padded_2(): lax.ppermute(lax.slice_in_dim(block, 0, width, axis=dim), axis, backward)  21.6 us
    sub x1, other arithmetic, attend_group(): probs = jax.nn.softmax(scores, axis=-1).astype(jnp.bfloat16)  19.1 us
    add x2, local copies, waits for them, and re-layouts, attend_group(): jnp.einsum('gqhd,gkhd->ghqk', qs, keys, preferred_element_type=jnp.float32)  18.8 us
    dot_general x1, matrix products, build_bias(): jnp.einsum('jqb,hipb->hijpq', selector, partial_rows, precision=lax.Preci...  18.2 us
    dot_general x1, matrix products, attend_group(): jnp.einsum('gqhd,gkhd->ghqk', qs, keys, preferred_element_type=jnp.float32)  7.14 us
    dot_general x1, matrix products, attend_group(): jnp.einsum('ghqk,gkhd->gqhd', probs, vals, preferred_element_type=jnp.flo...  6.31 us
  transfers between devices with their start and end apart: 16, of which 8 were waited for; matrix products, arithmetic and copies ran while one was open for 23% of the time, Pallas kernels for 0%

commit v1 on v0

v1 whole, which is shorter than its diff:
```python
import functools
import math

import jax
import jax.numpy as jnp
import numpy as np
from jax import lax
from jax.experimental import pallas as pl
from jax.experimental.pallas import tpu as pltpu
from jax.sharding import PartitionSpec as P

HEADS = 6
HEAD = 30
SLOT = 32
CH = 180
WIN = 16
KWIN = 24
SIDE = WIN + KWIN - 1
TABLE = SIDE * SIDE
TH = 16
TW = 64
PITCH = 80
GP = 72
QSCALE = math.log2(math.e) / math.sqrt(HEAD)
LOG2E = math.log2(math.e)
F32 = jnp.float32
BF16 = jnp.bfloat16
MESH = pl.DeviceIdType.MESH
NT = (((1,), (1,)), ((), ()))


def table_selector():
    out = np.zeros((5, 512, 384), np.float32)
    for tile in range(5):
        start = selector_start(tile)
        for lane in range(128):
            rev = 8 * tile + lane // 16
            if rev >= SIDE:
                continue
            for part in range(3):
                entry = 16 * part + lane % 16
                if entry < SIDE:
                    source = SIDE * (SIDE - 1 - rev) + SIDE - 1 - entry
                    out[tile, source - start, 128 * part + lane] = 1.0
    return out


def selector_start(tile):
    first = max(0, SIDE * (SIDE - 8 - 8 * tile))
    return min(first // 128 * 128, 1536 - 512)


def mm(a, b):
    return jnp.dot(a, b, preferred_element_type=F32)


def mm_nt(a, b):
    return lax.dot_general(a, b, NT, preferred_element_type=F32)


def iota(shape, dim):
    return lax.broadcasted_iota(jnp.int32, shape, dim)


def one_hot(mask):
    return jnp.where(mask, 1.0, 0.0).astype(BF16)


def normalize(x, gain):
    center = x - jnp.sum(x, axis=-1, keepdims=True) * (1.0 / CH)
    spread = jnp.sum(center * center, axis=-1, keepdims=True) * (1.0 / CH)
    return center * lax.rsqrt(spread + 1e-05) * gain


def kernel(
    nr, nc,
    feat, gain1, qkv, table, proj, gain2, hid, outw, gconv, bconv, uconv, selector,
    out,
    feat_v, gain1_v, qkv_v, table_v, proj_v, gain2_v, hid_v, outw_v, gconv_v, bconv_v, upad, sel_v,
    halo_t, halo_b, halo_l, halo_r, halo_c,
    mix_t, mix_b, mix_l, mix_r, mix_c, mix_own,
    fpad, npad, mixpad, gbuf, ybuf, lbuf, l3,
    qpad, wqt, wk, wvt, ppad, pw, hpad, opad, wout, gpad, bpad, w2, w3, bias, wrow, kwin, vwin, attt,
    local_sem, fsend, frecv, msend, mrecv,
):
    row = lax.axis_index("rows")
    col = lax.axis_index("cols")
    up = lax.rem(row + nr - 1, nr)
    down = lax.rem(row + 1, nr)
    left = lax.rem(col + nc - 1, nc)
    right = lax.rem(col + 1, nc)
    neighbours = [
        (up, col), (down, col), (row, left), (row, right),
        (up, left), (up, right), (down, left), (down, right),
    ]
    barrier = pltpu.get_barrier_semaphore()
    for target in neighbours:
        pl.semaphore_signal(barrier, inc=1, device_id=target, device_id_type=MESH)

    local = {}
    pairs = [
        ("feat", feat, feat_v), ("gain1", gain1, gain1_v), ("table", table, table_v),
        ("selector", selector, sel_v), ("qkv", qkv, qkv_v), ("proj", proj, proj_v),
        ("gain2", gain2, gain2_v), ("hid", hid, hid_v), ("outw", outw, outw_v),
        ("gconv", gconv, gconv_v), ("bconv", bconv, bconv_v), ("uconv", uconv, upad.at[:, 0:192, :]),
    ]
    for number, (name, source, target) in enumerate(pairs):
        local[name] = pltpu.make_async_copy(source, target, local_sem.at[number])
        local[name].start()

    def exchange(specs, send_sem, recv_sem):
        copies = []
        for number, (source, target, device) in enumerate(specs):
            copies.append(
                pltpu.make_async_remote_copy(
                    src_ref=source, dst_ref=target, send_sem=send_sem.at[number],
                    recv_sem=recv_sem.at[number], device_id=device, device_id_type=MESH,
                )
            )
        return copies

    fcopies = exchange(
        [
            (feat.at[0:4], halo_b, (up, col)),
            (feat.at[12:16], halo_t, (down, col)),
            (feat.at[:, 0:16], halo_r, (row, left)),
            (feat.at[:, 48:64], halo_l, (row, right)),
            (feat.at[0:4, 0:16], halo_c.at[3], (up, left)),
            (feat.at[0:4, 48:64], halo_c.at[2], (up, right)),
            (feat.at[12:16, 0:16], halo_c.at[1], (down, left)),
            (feat.at[12:16, 48:64], halo_c.at[0], (down, right)),
        ],
        fsend, frecv,
    )
    pl.semaphore_wait(barrier, 8)
    for copy in fcopies:
        copy.start()

    has_up = row > 0
    has_down = row < nr - 1
    has_left = col > 0
    has_right = col < nc - 1

    fpad[1] = jnp.zeros(fpad.shape[1:], F32)
    npad[1] = jnp.zeros(npad.shape[1:], F32)
    for ref in (qpad, ppad, hpad, opad, gpad, bpad):
        ref[...] = jnp.zeros(ref.shape, ref.dtype)
    for a in range(3):
        upad[a, 192:256, :] = jnp.zeros((64, 256), BF16)

    local["gain1"].wait()
    local["feat"].wait()
    g1 = gain1_v[...].reshape(1, CH)

    def store_pixels(start, count, values, valid=None):
        x = values.astype(F32)
        if valid is not None:
            x = jnp.where(valid, x, 0.0)
        n = normalize(x, g1)
        rows = pl.ds(start, count)
        fpad[0, rows, :] = x[:, 0:128]
        fpad[1, rows, 0:52] = x[:, 128:CH]
        npad[0, rows, :] = n[:, 0:128]
        npad[1, rows, 0:52] = n[:, 128:CH]

    def own_rows(h, carry):
        store_pixels(pl.multiple_of((h + 4) * PITCH + 8, 8), TW, feat_v[h])
        return carry

    lax.fori_loop(0, TH, own_rows, 0)

    local["qkv"].wait()
    qpad[0:CH, 0 : 3 * CH] = qkv_v[...]
    r = iota((256, 256), 0)
    c = iota((256, 256), 1)
    identity = one_hot(r == c)
    wqt[...] = (mm_nt(one_hot((r == c) & (r < CH)), qpad[:, 0:256]) * QSCALE).astype(F32)
    wk[...] = mm(qpad[:, 128:384], one_hot((r == c + 52) & (c < CH))).astype(BF16)
    rv = iota((192, 384), 0)
    cv = iota((192, 384), 1)
    slot_source = HEAD * lax.shift_right_logical(rv, 5) + (rv & 31)
    wvt[...] = mm_nt(one_hot((cv == slot_source + 104) & ((rv & 31) < HEAD)), qpad[:, 256:640]).astype(BF16)
    local["proj"].wait()
    ppad[0:CH, 0:CH] = proj_v[...]
    slot_source = HEAD * lax.shift_right_logical(r, 5) + (r & 31)
    pw[...] = mm(one_hot((c == slot_source) & ((r & 31) < HEAD) & (r < 192)), ppad[...]).astype(BF16)
    local["gain2"].wait()
    local["hid"].wait()
    hpad[0:CH, 0 : 2 * CH] = hid_v[...]
    local["outw"].wait()
    opad[0:CH, 0 : 2 * CH] = outw_v[...]
    wout[...] = mm_nt(one_hot(iota((384, 384), 0) == iota((384, 384), 1)), opad[...]).astype(BF16)
    local["gconv"].wait()
    for tap in range(9):
        gpad[tap, 0:CH, 0:CH] = gconv_v[tap // 3, tap % 3]
    local["bconv"].wait()
    local["uconv"].wait()
    order = 4 * (r & 63) + 2 * (lax.shift_right_logical(r, 6) & 1) + lax.shift_right_logical(r, 7)
    shuffle_rows = one_hot(c == order)
    for a in range(3):
        for b in range(3):
            bpad[a, 64 * b : 64 * (b + 1), 0:CH] = bconv_v[a, b]
        w2[a] = mm_nt(identity, bpad[a]).astype(BF16)
        w3[a] = mm_nt(shuffle_rows, upad[a]).astype(BF16)

    local["table"].wait()
    local["selector"].wait()
    whole = table_v[...] * LOG2E
    lane8 = iota((8, 128), 1)
    sub8 = iota((8, 128), 0)
    for tile in range(5):
        start = selector_start(tile)
        piece = whole[:, start : min(start + 512, TABLE)]
        sel = sel_v[tile, 0 : piece.shape[1], :]
        hi = piece.astype(BF16)
        rest = piece - hi.astype(F32)
        mid = rest.astype(BF16)
        low = (rest - mid.astype(F32)).astype(BF16)
        z = mm(hi, sel) + mm(mid, sel) + mm(low, sel)
        for group, (part, base) in enumerate(((1, 7), (0, 15), (0, 7))):
            use_first = (lane8 & 15) + base - sub8 < 16
            for head in range(HEADS):
                first = jnp.broadcast_to(z[head : head + 1, 128 * part : 128 * part + 128], (8, 128))
                second = jnp.broadcast_to(z[head : head + 1, 128 * part + 128 : 128 * part + 256], (8, 128))
                first = pltpu.roll(first, 128 - base, 1, stride=1, stride_axis=0)
                second = pltpu.roll(second, 16 - base, 1, stride=1, stride_axis=0)
                wrow[head, 8 * group : 8 * group + 8, 128 * tile : 128 * tile + 128] = jnp.where(
                    use_first, first, second
                )
    lane24 = iota((KWIN, 128), 1)

    def build_bias(head, carry):
        tiles = [wrow[head, :, 128 * k : 128 * k + 128] for k in range(5)]
        for shift in range(8):
            amount = 16 * shift
            if shift:
                rolled = [pltpu.roll(t, 128 - amount, 1) for t in tiles]
                joined = [
                    jnp.where(lane24 < 128 - amount, rolled[k], rolled[k + 1]) for k in range(4)
                ]
            else:
                joined = tiles
            for block in range(3):
                p = KWIN - 1 - 8 * block - shift
                for half in range(2):
                    bias[head, KWIN * p : KWIN * (p + 1), 128 * half : 128 * half + 128] = joined[
                        block + half
                    ]
        return carry

    lax.fori_loop(0, HEADS, build_bias, 0)

    for copy in fcopies:
        copy.wait_recv()

    def halo_rows(h, carry):
        for ref, first, valid, kinds in ((halo_t, 0, has_up, (0, 1)), (halo_b, 20, has_down, (2, 3))):
            start = (first + h) * PITCH
            store_pixels(pl.multiple_of(start + 8, 8), TW, ref[h], valid)
            lo = halo_c[kinds[0], h].astype(F32)[8:16]
            hi = halo_c[kinds[1], h].astype(F32)[0:8]
            store_pixels(pl.multiple_of(start, 8), 8, lo, valid & has_left)
            store_pixels(pl.multiple_of(start + 72, 8), 8, hi, valid & has_right)
        return carry

    lax.fori_loop(0, 4, halo_rows, 0)

    def halo_cols(h, carry):
        start = (4 + h) * PITCH
        store_pixels(pl.multiple_of(start, 8), 8, halo_l[h].astype(F32)[8:16], has_left)
        store_pixels(pl.multiple_of(start + 72, 8), 8, halo_r[h].astype(F32)[0:8], has_right)
        return carry

    lax.fori_loop(0, TH, halo_cols, 0)

    g2 = jnp.concatenate([gain2_v[...].reshape(1, CH), jnp.zeros((1, 256 - CH), F32)], axis=1)
    chan = iota((256, 256), 1)
    inside = chan < CH
    ones_row = (iota((192, KWIN * KWIN), 0) & 31) == HEAD

    def window(w, carry):
        def pixels(ref, half, first_row, count_rows, first_col, count_cols):
            return jnp.concatenate(
                [
                    ref[half, pl.ds((first_row + p) * PITCH + first_col + w * WIN, count_cols), :]
                    for p in range(count_rows)
                ],
                axis=0,
            )

        keys_in = jnp.concatenate(
            [pixels(npad, half, 0, KWIN, 4, KWIN).astype(BF16) for half in range(2)], axis=1
        )
        kwin[...] = mm(keys_in, wk[...]).astype(BF16)
        values = mm_nt(wvt[...], keys_in)
        vwin[...] = jnp.where(ones_row, 1.0, values).astype(BF16)
        query_in = jnp.concatenate(
            [pixels(npad, half, 4, WIN, 8, WIN).astype(BF16) for half in range(2)], axis=1
        )
        queries = mm_nt(wqt[...].astype(BF16), query_in)
        for head in range(HEADS):
            mine = (r >= HEAD * head) & (r < HEAD * (head + 1))
            q = jnp.where(mine, queries, 0.0).astype(BF16)
            scores = mm(kwin[...], q) + bias[head]
            top = jnp.max(scores, axis=0, keepdims=True)
            probs = jnp.exp2(scores - top).astype(BF16)
            mixed_values = mm(vwin[SLOT * head : SLOT * (head + 1), :], probs)
            total = mixed_values[HEAD : HEAD + 1, :]
            attt[SLOT * head : SLOT * (head + 1), :] = (mixed_values / total).astype(BF16)
        attended = mm_nt(identity, attt[...]).astype(BF16)
        base = jnp.concatenate([pixels(fpad, half, 4, WIN, 8, WIN) for half in range(2)], axis=1)
        first = base + mm(attended, pw[0:192, :])
        center = first - jnp.sum(first, axis=-1, keepdims=True) * (1.0 / CH)
        center = jnp.where(inside, center, 0.0)
        spread = jnp.sum(center * center, axis=-1, keepdims=True) * (1.0 / CH)
        second = (center * lax.rsqrt(spread + 1e-05) * g2).astype(BF16)
        inner = mm(second, hpad[...])
        inner = (0.5 * inner * (1.0 + lax.erf(inner * math.sqrt(0.5)))).astype(BF16)
        mixed = first + mm(inner, wout[...])
        for i in range(WIN):
            block = mixed[WIN * i : WIN * (i + 1), :]
            rows = pl.ds(pl.multiple_of((3 + i) * PITCH + 8 + w * WIN, 8), WIN)
            mixpad[0, rows, :] = block[:, 0:128]
            mixpad[1, rows, :] = block[:, 128:256]
            mix_own[i, pl.ds(pl.multiple_of(w * WIN, WIN), WIN), :] = block.astype(BF16)
        return carry

    lax.fori_loop(0, TW // WIN, window, 0)

    mcopies = exchange(
        [
            (mix_own.at[0:3], mix_b, (up, col)),
            (mix_own.at[13:16], mix_t, (down, col)),
            (mix_own.at[:, 0:16], mix_r, (row, left)),
            (mix_own.at[:, 48:64], mix_l, (row, right)),
            (mix_own.at[0:3, 0:16], mix_c.at[3], (up, left)),
            (mix_own.at[0:3, 48:64], mix_c.at[2], (up, right)),
            (mix_own.at[13:16, 0:16], mix_c.at[1], (down, left)),
            (mix_own.at[13:16, 48:64], mix_c.at[0], (down, right)),
        ],
        msend, mrecv,
    )
    for copy in mcopies:
        copy.start()
    for copy in mcopies:
        copy.wait_recv()

    def store_mixed(start, count, values, valid):
        x = jnp.where(valid, values.astype(F32), 0.0)
        rows = pl.ds(start, count)
        mixpad[0, rows, :] = x[:, 0:128]
        mixpad[1, rows, :] = x[:, 128:256]

    for h in range(3):
        for ref, first, valid, kinds in ((mix_t, 0, has_up, (0, 1)), (mix_b, 19, has_down, (2, 3))):
            start = (first + h) * PITCH
            store_mixed(start + 8, TW, ref[h], valid)
            store_mixed(start, 8, mix_c[kinds[0], h].astype(F32)[8:16], valid & has_left)
            store_mixed(start + 72, 8, mix_c[kinds[1], h].astype(F32)[0:8], valid & has_right)
    for h in range(TH):
        start = (3 + h) * PITCH
        store_mixed(start, 8, mix_l[h].astype(F32)[8:16], has_left)
        store_mixed(start + 72, 8, mix_r[h].astype(F32)[0:8], has_right)

    cols72 = iota((GP, 128), 0)
    gcols = ((cols72 >= 2) | has_left) & ((cols72 < 66) | has_right)

    def conv_group(step, carry):
        h0 = step * 4
        acc = None
        for a in range(3):
            for b in range(3):
                halves = []
                for half in range(2):
                    rows = [
                        mixpad[half, pl.ds((h0 + k + a) * PITCH + 5 + b, GP), :] for k in range(4)
                    ]
                    halves.append(jnp.concatenate(rows, axis=0).astype(BF16))
                term = mm(jnp.concatenate(halves, axis=1), gpad[3 * a + b])
                acc = term if acc is None else acc + term
        for k in range(4):
            h = h0 + k
            keep = gcols & ((h >= 2) | has_up) & ((h < 18) | has_down)
            for half in range(2):
                base = fpad[half, pl.ds((h + 2) * PITCH + 6, GP), :]
                value = base + acc[GP * k : GP * (k + 1), 128 * half : 128 * half + 128]
                gbuf[half, pl.ds(pl.multiple_of(h * GP, 8), GP), :] = jnp.where(keep, value, 0.0)
        return carry

    lax.fori_loop(0, 5, conv_group, 0)

    def conv_before(step, carry):
        start = pl.multiple_of(step * (6 * GP), 16)
        acc = None
        for a in range(3):
            rows = pl.ds(pl.multiple_of(start + a * GP, 8), 6 * GP)
            lhs = jnp.concatenate([gbuf[half, rows, :].astype(BF16) for half in range(2)], axis=1)
            term = mm(lhs, w2[a])
            acc = term if acc is None else acc + term
        rows = pl.ds(start, 6 * GP)
        ybuf[0, rows, :] = acc[:, 0:128]
        ybuf[1, rows, :] = acc[:, 128:256]
        return carry

    ybuf[:, 18 * GP :, :] = jnp.zeros((2, 8, 128), F32)
    lbuf[18 * GP :, :] = jnp.zeros((8, 128), F32)
    lax.fori_loop(0, 3, conv_before, 0)
    lcols = ((cols72 >= 1) | has_left) & ((cols72 < 65) | has_right)
    low_lanes = iota((GP, 128), 1) < 64

    def finish_before(h, carry):
        start = h * GP
        value = (
            ybuf[0, pl.ds(pl.multiple_of(start, 8), GP), :]
            + pltpu.roll(ybuf[0, pl.ds(start + 1, GP), :], 64, 1)
            + ybuf[1, pl.ds(start + 2, GP), :]
        )
        value = jnp.where(value >= 0, value, 0.01 * value)
        value = jnp.where(lcols & ((h >= 1) | has_up) & ((h < 17) | has_down), value, 0.0)
        lbuf[pl.ds(pl.multiple_of(start, 8), GP), :] = jnp.where(
            low_lanes, value, pltpu.roll(value, 64, 1)
        )
        return carry

    lax.fori_loop(0, 18, finish_before, 0)
    low64 = iota((TW, 128), 1) < 64

    def gather_taps(h, carry):
        start = h * GP
        zero = lbuf[pl.ds(pl.multiple_of(start, 8), TW), :]
        one = lbuf[pl.ds(start + 1, TW), :]
        two = lbuf[pl.ds(start + 2, TW), :]
        l3[h, :, 0:128] = jnp.where(low64, zero, one).astype(BF16)
        l3[h, :, 128:256] = jnp.where(low64, two, 0.0).astype(BF16)
        return carry

    lax.fori_loop(0, 18, gather_taps, 0)

    target = 128 * (lax.shift_right_logical(r, 6) & 1) + 2 * (r & 63) + lax.shift_right_logical(r, 7)
    weave = one_hot(c == target)

    def conv_up(step, carry):
        acc = None
        for a in range(3):
            rhs = jnp.concatenate([l3[4 * step + a + k] for k in range(4)], axis=0)
            term = mm_nt(w3[a], rhs)
            acc = term if acc is None else acc + term
        acc = acc.astype(BF16)
        for pair in range(2):
            lanes = slice(128 * pair, 128 * pair + 128)
            both = jnp.concatenate([acc[0:128, lanes], acc[128:256, lanes]], axis=1)
            woven = mm(both, weave).astype(BF16)
            for k in range(2):
                for a in range(2):
                    out[2 * (4 * step + 2 * pair + k) + a] = woven[
                        64 * a : 64 * (a + 1), 128 * k : 128 * k + 128
                    ]
        return carry

    lax.fori_loop(0, 4, conv_up, 0)
    for copy in fcopies + mcopies:
        copy.wait_send()


def on_device(
    nr, nc, features, gain_one, qkv_weight, bias_table, proj_weight, gain_two,
    hidden_weight, output_weight, group_conv, before_conv, upsample_conv,
):
    selector = jnp.asarray(table_selector(), BF16)
    operands = (
        features, gain_one, qkv_weight, bias_table.T, proj_weight, gain_two, hidden_weight,
        output_weight.T, group_conv, before_conv.transpose(0, 1, 3, 2),
        upsample_conv.reshape(3, 192, 256), selector,
    )
    any_space = pl.BlockSpec(memory_space=pl.ANY)
    staged = [pltpu.VMEM(x.shape, x.dtype) for x in operands]
    staged[10] = pltpu.VMEM((3, 256, 256), BF16)
    scratch = staged + [
        pltpu.VMEM((4, TW, CH), BF16), pltpu.VMEM((4, TW, CH), BF16),
        pltpu.VMEM((TH, 16, CH), BF16), pltpu.VMEM((TH, 16, CH), BF16),
        pltpu.VMEM((4, 4, 16, CH), BF16),
        pltpu.VMEM((3, TW, 256), BF16), pltpu.VMEM((3, TW, 256), BF16),
        pltpu.VMEM((TH, 16, 256), BF16), pltpu.VMEM((TH, 16, 256), BF16),
        pltpu.VMEM((4, 3, 16, 256), BF16), pltpu.VMEM((TH, TW, 256), BF16),
        pltpu.VMEM((2, 24 * PITCH, 128), F32), pltpu.VMEM((2, 24 * PITCH, 128), F32),
        pltpu.VMEM((2, 22 * PITCH, 128), F32), pltpu.VMEM((2, 20 * GP, 128), F32),
        pltpu.VMEM((2, 18 * GP + 8, 128), F32), pltpu.VMEM((18 * GP + 8, 128), F32),
        pltpu.VMEM((18, TW, 256), BF16),
        pltpu.VMEM((256, 640), BF16), pltpu.VMEM((256, 256), F32), pltpu.VMEM((256, 256), BF16),
        pltpu.VMEM((192, 256), BF16), pltpu.VMEM((256, 256), BF16), pltpu.VMEM((256, 256), BF16),
        pltpu.VMEM((256, 384), BF16), pltpu.VMEM((256, 384), BF16), pltpu.VMEM((384, 256), BF16),
        pltpu.VMEM((9, 256, 256), BF16), pltpu.VMEM((3, 256, 256), BF16),
        pltpu.VMEM((3, 256, 256), BF16), pltpu.VMEM((3, 256, 256), BF16),
        pltpu.VMEM((HEADS, KWIN * KWIN, 256), F32), pltpu.VMEM((HEADS, KWIN, 640), F32),
        pltpu.VMEM((KWIN * KWIN, 256), BF16), pltpu.VMEM((192, KWIN * KWIN), BF16),
        pltpu.VMEM((192, 256), BF16),
        pltpu.SemaphoreType.DMA((12,)), pltpu.SemaphoreType.DMA((8,)), pltpu.SemaphoreType.DMA((8,)),
        pltpu.SemaphoreType.DMA((8,)), pltpu.SemaphoreType.DMA((8,)),
    ]
    result = pl.pallas_call(
        functools.partial(kernel, nr, nc),
        out_shape=jax.ShapeDtypeStruct((2 * TH, 64, 2 * TW), BF16),
        in_specs=[any_space] * len(operands),
        out_specs=pl.BlockSpec(memory_space=pltpu.VMEM),
        scratch_shapes=scratch,
        compiler_params=pltpu.CompilerParams(
            collective_id=0, has_side_effects=True, vmem_limit_bytes=48 * 1024 * 1024
        ),
    )(*operands)
    return result.transpose(1, 0, 2)


def solution(mesh):
    placed = (P("rows", "cols", None),) + (P(),) * 10
    body = functools.partial(on_device, mesh.shape["rows"], mesh.shape["cols"])
    return jax.shard_map(
        body, mesh=mesh, in_specs=placed, out_specs=P(None, "rows", "cols"), check_vma=False
    )
```

time: 194 us -> 64.1 us (0.33)
  the two profiles are of different devices: /device:TPU:103 before, /device:TPU:1 now
where the time goes in v1:
time: 64.1 us; the launch traced here: 63.6 us
  Pallas kernels  51 us (80%)
  local copies, waits for them, and re-layouts  12.6 us (20%)
    pallas_call x1, Pallas kernels, on_device(): pl.pallas_call(functools.partial(kernel, nr, nc), out_shape=jax.ShapeDtyp...  51 us
    unnamed x24, local copies, waits for them, and re-layouts  11.5 us

profile of v1, /device:TPU:1, one launch (start us, length us, event | category | flops | bytes accessed | tf_op | source)
XLA Modules:
  0.0 63.6 jit_solution(16051518643838496643)
XLA Ops:
  0.0 0.0 copy-start
  0.0 1.5 %copy-done = bf16[5,512,384]{2,1,0:T(8,128)(2,1)S(1)} copy-done((bf16[5,512,384]{2,1,0:T(8,128)(2,1)S(1)}, bf16[5,512,384]{2,1,0:T(8,128)(2,1)}, u32[]{:S(2)}) %copy-start) | copy-done | bytes 1966104
  1.5 0.0 copy-start.1
  1.5 1.2 %copy-done.1 = bf16[3,3,180,180]{3,2,1,0:T(8,128)(2,1)S(1)} copy-done((bf16[3,3,180,180]{3,2,1,0:T(8,128)(2,1)S(1)}, bf16[3,3,180,180]{3,2,1,0:T(8,128)(2,1)}, u32[]{:S(2)}) %copy-start.1) | copy-done | bytes 583224
  2.7 0.0 copy-start.2
  2.7 1.0 %copy-done.2 = bf16[16,64,180]{2,1,0:T(8,128)(2,1)S(1)} copy-done((bf16[16,64,180]{2,1,0:T(8,128)(2,1)S(1)}, bf16[16,64,180]{2,1,0:T(8,128)(2,1)}, u32[]{:S(2)}) %copy-start.2) | copy-done | bytes 368664
  3.7 0.0 copy-start.3
  3.7 1.0 %copy-done.3 = bf16[3,3,180,64]{2,3,1,0:T(8,128)(2,1)S(1)} copy-done((bf16[3,3,180,64]{2,3,1,0:T(8,128)(2,1)S(1)}, bf16[3,3,180,64]{2,3,1,0:T(8,128)(2,1)}, u32[]{:S(2)}) %copy-start.3) | copy-done | bytes 207384
  4.7 0.0 copy-start.4
  4.7 1.0 %copy-done.4 = bf16[3,3,64,256]{3,2,1,0:T(8,128)(2,1)S(1)} copy-done((bf16[3,3,64,256]{3,2,1,0:T(8,128)(2,1)S(1)}, bf16[3,3,64,256]{3,2,1,0:T(8,128)(2,1)}, u32[]{:S(2)}) %copy-start.4) | copy-done | bytes 294936
  5.7 0.0 copy-start.5
  5.7 0.9 %copy-done.5 = bf16[180,540]{1,0:T(8,128)(2,1)S(1)} copy-done((bf16[180,540]{1,0:T(8,128)(2,1)S(1)}, bf16[180,540]{1,0:T(8,128)(2,1)}, u32[]{:S(2)}) %copy-start.5) | copy-done | bytes 194424
  6.6 0.0 copy-start.6
  6.6 0.9 %copy-done.6 = bf16[180,360]{1,0:T(8,128)(2,1)S(1)} copy-done((bf16[180,360]{1,0:T(8,128)(2,1)S(1)}, bf16[180,360]{1,0:T(8,128)(2,1)}, u32[]{:S(2)}) %copy-start.6) | copy-done | bytes 129624
  7.5 0.0 copy-start.7
  7.5 0.9 %copy-done.7 = bf16[360,180]{0,1:T(8,128)(2,1)S(1)} copy-done((bf16[360,180]{0,1:T(8,128)(2,1)S(1)}, bf16[360,180]{0,1:T(8,128)(2,1)}, u32[]{:S(2)}) %copy-start.7) | copy-done | bytes 129624
  8.4 0.0 copy-start.8
  8.4 0.9 %copy-done.8 = bf16[180,180]{1,0:T(8,128)(2,1)S(1)} copy-done((bf16[180,180]{1,0:T(8,128)(2,1)S(1)}, bf16[180,180]{1,0:T(8,128)(2,1)}, u32[]{:S(2)}) %copy-start.8) | copy-done | bytes 64824
  9.3 0.0 copy-start.9
  9.3 0.8 %copy-done.9 = f32[1521,6]{0,1:T(8,128)S(1)} copy-done((f32[1521,6]{0,1:T(8,128)S(1)}, f32[1521,6]{0,1:T(8,128)}, u32[]{:S(2)}) %copy-start.9) | copy-done | bytes 36528
  10.1 0.7 %copy-done.10 = f32[180]{0:T(256)S(1)} copy-done((f32[180]{0:T(256)S(1)}, f32[180]{0:T(256)}, u32[]{:S(2)}) %copy-start.10) | copy-done | bytes 744
  10.8 0.7 %copy-done.11 = f32[180]{0:T(256)S(1)} copy-done((f32[180]{0:T(256)S(1)}, f32[180]{0:T(256)}, u32[]{:S(2)}) %copy-start.11) | copy-done | bytes 744
  11.5 51.0 %shard_map.118 = bf16[32,64,128]{2,1,0:T(8,128)(2,1)S(1)} custom-call(bf16[16,64,180]{2,1,0:T(8,128)(2,1)S(1)} %copy-done.2, f32[180]{0:T(256)S(1)} %copy-done.10, bf16[180,540]{1,0:T(8,128)(2,1)S(1)} %copy-done.5, f32[6,1521]{1,0:T(8,128)S(1)} %bitcast.9, bf16[180,180]{1,0:T(8,128)(2,1)S(1)} %copy-done.8, f32[180]{0:T(256)S(1)} %copy-done.11, ...), custom_call_target="tpu_custom_call" | custom-call | tf_op jit(solution)/shard_map/pallas_call | solution.py:500
  62.5 1.1 %copy.13 = bf16[64,32,128]{2,1,0:T(8,128)(2,1)} copy(bf16[64,32,128]{2,0,1:T(8,128)(2,1)S(1)} %bitcast.5) | data formatting | bytes 1048576 | tf_op jit(solution)/shard_map/transpose | solution.py:510
  (2 shorter events, 0.0 us)
Async XLA Ops:
  0.0 1.5 %copy-start = (bf16[5,512,384]{2,1,0:T(8,128)(2,1)S(1)}, bf16[5,512,384]{2,1,0:T(8,128)(2,1)}, u32[]{:S(2)}) copy-start(bf16[5,512,384]{2,1,0:T(8,128)(2,1)} %constant.2.clone.selector) | copy-start | bytes 5898244
  1.5 1.2 %copy-start.1 = (bf16[3,3,180,180]{3,2,1,0:T(8,128)(2,1)S(1)}, bf16[3,3,180,180]{3,2,1,0:T(8,128)(2,1)}, u32[]{:S(2)}) copy-start(bf16[3,3,180,180]{3,2,1,0:T(8,128)(2,1)} %gconv.1) | copy-start | bytes 1749604
  2.7 1.0 %copy-start.2 = (bf16[16,64,180]{2,1,0:T(8,128)(2,1)S(1)}, bf16[16,64,180]{2,1,0:T(8,128)(2,1)}, u32[]{:S(2)}) copy-start(bf16[16,64,180]{2,1,0:T(8,128)(2,1)} %feat.1) | copy-start | bytes 1105924
  3.7 1.0 %copy-start.3 = (bf16[3,3,180,64]{2,3,1,0:T(8,128)(2,1)S(1)}, bf16[3,3,180,64]{2,3,1,0:T(8,128)(2,1)}, u32[]{:S(2)}) copy-start(bf16[3,3,180,64]{2,3,1,0:T(8,128)(2,1)} %param.21) | copy-start | bytes 622084
  4.7 1.0 %copy-start.4 = (bf16[3,3,64,256]{3,2,1,0:T(8,128)(2,1)S(1)}, bf16[3,3,64,256]{3,2,1,0:T(8,128)(2,1)}, u32[]{:S(2)}) copy-start(bf16[3,3,64,256]{3,2,1,0:T(8,128)(2,1)} %param.22) | copy-start | bytes 884740
  5.7 0.9 %copy-start.5 = (bf16[180,540]{1,0:T(8,128)(2,1)S(1)}, bf16[180,540]{1,0:T(8,128)(2,1)}, u32[]{:S(2)}) copy-start(bf16[180,540]{1,0:T(8,128)(2,1)} %qkv.1) | copy-start | bytes 583204
  6.6 0.9 %copy-start.6 = (bf16[180,360]{1,0:T(8,128)(2,1)S(1)}, bf16[180,360]{1,0:T(8,128)(2,1)}, u32[]{:S(2)}) copy-start(bf16[180,360]{1,0:T(8,128)(2,1)} %hid.1) | copy-start | bytes 388804
  7.5 0.9 %copy-start.7 = (bf16[360,180]{0,1:T(8,128)(2,1)S(1)}, bf16[360,180]{0,1:T(8,128)(2,1)}, u32[]{:S(2)}) copy-start(bf16[360,180]{0,1:T(8,128)(2,1)} %param.19) | copy-start | bytes 388804
  8.4 0.9 %copy-start.8 = (bf16[180,180]{1,0:T(8,128)(2,1)S(1)}, bf16[180,180]{1,0:T(8,128)(2,1)}, u32[]{:S(2)}) copy-start(bf16[180,180]{1,0:T(8,128)(2,1)} %proj.1) | copy-start | bytes 194404
  9.3 0.8 %copy-start.9 = (f32[1521,6]{0,1:T(8,128)S(1)}, f32[1521,6]{0,1:T(8,128)}, u32[]{:S(2)}) copy-start(f32[1521,6]{0,1:T(8,128)} %param.15) | copy-start | bytes 109516
  10.1 0.7 %copy-start.10 = (f32[180]{0:T(256)S(1)}, f32[180]{0:T(256)}, u32[]{:S(2)}) copy-start(f32[180]{0:T(256)} %gain1.1) | copy-start | bytes 2164
  10.8 0.7 %copy-start.11 = (f32[180]{0:T(256)S(1)}, f32[180]{0:T(256)}, u32[]{:S(2)}) copy-start(f32[180]{0:T(256)} %gain2.1) | copy-start | bytes 2164

commit v2 on v1

v2 whole, which is shorter than its diff:
```python
import functools
import math

import jax
import jax.numpy as jnp
import numpy as np
from jax import lax
from jax.experimental import pallas as pl
from jax.experimental.pallas import tpu as pltpu
from jax.sharding import PartitionSpec as P

HEADS = 6
HEAD = 30
SLOT = 32
CH = 180
WIN = 16
KWIN = 24
SIDE = WIN + KWIN - 1
TABLE = SIDE * SIDE
TH = 16
TW = 64
PITCH = 80
GP = 72
QSCALE = math.log2(math.e) / math.sqrt(HEAD)
LOG2E = math.log2(math.e)
F32 = jnp.float32
BF16 = jnp.bfloat16
MESH = pl.DeviceIdType.MESH
NT = (((1,), (1,)), ((), ()))


def table_selector():
    out = np.zeros((5, 512, 384), np.float32)
    for tile in range(5):
        start = selector_start(tile)
        for lane in range(128):
            rev = 8 * tile + lane // 16
            if rev >= SIDE:
                continue
            for part in range(3):
                entry = 16 * part + lane % 16
                if entry < SIDE:
                    source = SIDE * (SIDE - 1 - rev) + SIDE - 1 - entry
                    out[tile, source - start, 128 * part + lane] = 1.0
    return out


def selector_start(tile):
    first = max(0, SIDE * (SIDE - 8 - 8 * tile))
    return min(first // 128 * 128, 1536 - 512)


def mm(a, b):
    return jnp.dot(a, b, preferred_element_type=F32)


def mm_nt(a, b):
    return lax.dot_general(a, b, NT, preferred_element_type=F32)


def iota(shape, dim):
    return lax.broadcasted_iota(jnp.int32, shape, dim)


def one_hot(mask):
    return jnp.where(mask, 1.0, 0.0).astype(BF16)


def normalize(x, gain):
    center = x - jnp.sum(x, axis=-1, keepdims=True) * (1.0 / CH)
    spread = jnp.sum(center * center, axis=-1, keepdims=True) * (1.0 / CH)
    return center * lax.rsqrt(spread + 1e-05) * gain


def kernel(
    nr, nc,
    feat, gain1, qkv, table, proj, gain2, hid, outw, gconv, bconv, uconv, selector,
    out,
    feat_v, gain1_v, qkv_v, table_v, proj_v, gain2_v, hid_v, outw_v, gconv_v, bconv_v, upad, sel_v,
    halo_t, halo_b, halo_l, halo_r, halo_c,
    mix_t, mix_b, mix_l, mix_r, mix_c, mix_own,
    fpad, npad, mixpad, gbuf, ybuf, lbuf, l3,
    qpad, wqt, wk, wvt, ppad, pw, hpad, opad, wout, gpad, bpad, w2, w3, bias, wrow, kwin, vwin, qwin, sbuf, pbuf, attt, obuf,
    local_sem, fsend, frecv, msend, mrecv,
):
    row = lax.axis_index("rows")
    col = lax.axis_index("cols")
    up = lax.rem(row + nr - 1, nr)
    down = lax.rem(row + 1, nr)
    left = lax.rem(col + nc - 1, nc)
    right = lax.rem(col + 1, nc)
    neighbours = [
        (up, col), (down, col), (row, left), (row, right),
        (up, left), (up, right), (down, left), (down, right),
    ]
    barrier = pltpu.get_barrier_semaphore()
    for target in neighbours:
        pl.semaphore_signal(barrier, inc=1, device_id=target, device_id_type=MESH)

    local = {}
    pairs = [
        ("feat", feat, feat_v), ("gain1", gain1, gain1_v), ("table", table, table_v),
        ("selector", selector, sel_v), ("qkv", qkv, qkv_v), ("proj", proj, proj_v),
        ("gain2", gain2, gain2_v), ("hid", hid, hid_v), ("outw", outw, outw_v),
        ("gconv", gconv, gconv_v), ("bconv", bconv, bconv_v), ("uconv", uconv, upad.at[:, 0:192, :]),
    ]
    for number, (name, source, target) in enumerate(pairs):
        local[name] = pltpu.make_async_copy(source, target, local_sem.at[number])
        local[name].start()

    def arrive(*names):
        for name in names:
            local[name].wait()

    def exchange(specs, send_sem, recv_sem):
        copies = []
        for number, (source, target, device) in enumerate(specs):
            copies.append(
                pltpu.make_async_remote_copy(
                    src_ref=source, dst_ref=target, send_sem=send_sem.at[number],
                    recv_sem=recv_sem.at[number], device_id=device, device_id_type=MESH,
                )
            )
        return copies

    fcopies = exchange(
        [
            (feat.at[0:4], halo_b, (up, col)),
            (feat.at[12:16], halo_t, (down, col)),
            (feat.at[:, 0:16], halo_r, (row, left)),
            (feat.at[:, 48:64], halo_l, (row, right)),
            (feat.at[0:4, 0:16], halo_c.at[3], (up, left)),
            (feat.at[0:4, 48:64], halo_c.at[2], (up, right)),
            (feat.at[12:16, 0:16], halo_c.at[1], (down, left)),
            (feat.at[12:16, 48:64], halo_c.at[0], (down, right)),
        ],
        fsend, frecv,
    )
    pl.semaphore_wait(barrier, 8)
    for copy in fcopies:
        copy.start()

    has_up = row > 0
    has_down = row < nr - 1
    has_left = col > 0
    has_right = col < nc - 1

    fpad[1] = jnp.zeros(fpad.shape[1:], F32)
    npad[1] = jnp.zeros(npad.shape[1:], F32)
    for ref in (qpad, ppad, hpad, opad, gpad, bpad):
        ref[...] = jnp.zeros(ref.shape, ref.dtype)
    for a in range(3):
        upad[a, 192:256, :] = jnp.zeros((64, 256), BF16)

    arrive("gain1", "feat")
    g1 = gain1_v[...].reshape(1, CH)

    def store_pixels(x, starts):
        n = normalize(x, g1)
        width = x.shape[0] // len(starts)
        for k, start in enumerate(starts):
            part = slice(k * width, (k + 1) * width)
            rows = pl.ds(start, width)
            fpad[0, rows, :] = x[part, 0:128]
            fpad[1, rows, 0:52] = x[part, 128:CH]
            npad[0, rows, :] = n[part, 0:128]
            npad[1, rows, 0:52] = n[part, 128:CH]

    def own_pixels():
        for h in range(0, TH, 4):
            x = feat_v[h : h + 4].astype(F32).reshape(4 * TW, CH)
            store_pixels(x, [(h + k + 4) * PITCH + 8 for k in range(4)])

    own_pixels()
    r = iota((256, 256), 0)
    c = iota((256, 256), 1)
    identity = one_hot(r == c)

    def prepare_weights():
        qpad[0:CH, 0 : 3 * CH] = qkv_v[...]
        wqt[...] = mm_nt(one_hot((r == c) & (r < CH)), qpad[:, 0:256]).astype(BF16)
        wk[...] = mm(qpad[:, 128:384], one_hot((r == c + 52) & (c < CH))).astype(BF16)
        rv = iota((192, 384), 0)
        cv = iota((192, 384), 1)
        slot_source = HEAD * lax.shift_right_logical(rv, 5) + (rv & 31)
        wvt[...] = mm_nt(one_hot((cv == slot_source + 104) & ((rv & 31) < HEAD)), qpad[:, 256:640]).astype(BF16)
        ppad[0:CH, 0:CH] = proj_v[...]
        slot_source = HEAD * lax.shift_right_logical(r, 5) + (r & 31)
        pw[...] = mm(one_hot((c == slot_source) & ((r & 31) < HEAD) & (r < 192)), ppad[...]).astype(BF16)
        hpad[0:CH, 0 : 2 * CH] = hid_v[...]
        opad[0:CH, 0 : 2 * CH] = outw_v[...]
        wout[...] = mm_nt(one_hot(iota((384, 384), 0) == iota((384, 384), 1)), opad[...]).astype(BF16)
        for tap in range(9):
            gpad[tap, 0:CH, 0:CH] = gconv_v[tap // 3, tap % 3]
        order = 4 * (r & 63) + 2 * (lax.shift_right_logical(r, 6) & 1) + lax.shift_right_logical(r, 7)
        shuffle_rows = one_hot(c == order)
        for a in range(3):
            for b in range(3):
                bpad[a, 64 * b : 64 * (b + 1), 0:CH] = bconv_v[a, b]
            w2[a] = mm_nt(identity, bpad[a]).astype(BF16)
            w3[a] = mm_nt(shuffle_rows, upad[a]).astype(BF16)

    arrive("qkv", "proj", "gain2", "hid", "outw", "gconv", "bconv", "uconv")
    prepare_weights()
    def prepare_bias():
        whole = table_v[...] * LOG2E
        lane8 = iota((8, 128), 1)
        sub8 = iota((8, 128), 0)
        for tile in range(5):
            start = selector_start(tile)
            piece = whole[:, start : min(start + 512, TABLE)]
            sel = sel_v[tile, 0 : piece.shape[1], :]
            hi = piece.astype(BF16)
            rest = piece - hi.astype(F32)
            mid = rest.astype(BF16)
            low = (rest - mid.astype(F32)).astype(BF16)
            z = mm(hi, sel) + mm(mid, sel) + mm(low, sel)
            for group, (part, base) in enumerate(((1, 7), (0, 15), (0, 7))):
                use_first = (lane8 & 15) + base - sub8 < 16
                for head in range(HEADS):
                    first = jnp.broadcast_to(z[head : head + 1, 128 * part : 128 * part + 128], (8, 128))
                    second = jnp.broadcast_to(z[head : head + 1, 128 * part + 128 : 128 * part + 256], (8, 128))
                    first = pltpu.roll(first, 128 - base, 1, stride=1, stride_axis=0)
                    second = pltpu.roll(second, 16 - base, 1, stride=1, stride_axis=0)
                    wrow[head, 8 * group : 8 * group + 8, 128 * tile : 128 * tile + 128] = jnp.where(
                        use_first, first, second
                    )
        lane24 = iota((KWIN, 128), 1)

        def build_bias(head, carry):
            tiles = [wrow[head, :, 128 * k : 128 * k + 128] for k in range(5)]
            for shift in range(8):
                amount = 16 * shift
                if shift:
                    rolled = [pltpu.roll(t, 128 - amount, 1) for t in tiles]
                    joined = [
                        jnp.where(lane24 < 128 - amount, rolled[k], rolled[k + 1]) for k in range(4)
                    ]
                else:
                    joined = tiles
                for block in range(3):
                    p = KWIN - 1 - 8 * block - shift
                    for half in range(2):
                        bias[head, KWIN * p : KWIN * (p + 1), 128 * half : 128 * half + 128] = joined[
                            block + half
                        ]
            return carry

        lax.fori_loop(0, HEADS, build_bias, 0)

    arrive("table", "selector")
    prepare_bias()
    def halo_pixels():
        for ref, first, valid, kinds in ((halo_t, 0, has_up, (0, 1)), (halo_b, 20, has_down, (2, 3))):
            x = jnp.where(valid, ref[...].astype(F32).reshape(4 * TW, CH), 0.0)
            store_pixels(x, [(first + h) * PITCH + 8 for h in range(4)])
            lo = halo_c[kinds[0]].astype(F32)[:, 8:16, :].reshape(32, CH)
            hi = halo_c[kinds[1]].astype(F32)[:, 0:8, :].reshape(32, CH)
            store_pixels(
                jnp.where(valid & has_left, lo, 0.0), [(first + h) * PITCH for h in range(4)]
            )
            store_pixels(
                jnp.where(valid & has_right, hi, 0.0), [(first + h) * PITCH + 72 for h in range(4)]
            )
        lo = halo_l[...].astype(F32)[:, 8:16, :].reshape(8 * TH, CH)
        hi = halo_r[...].astype(F32)[:, 0:8, :].reshape(8 * TH, CH)
        store_pixels(jnp.where(has_left, lo, 0.0), [(4 + h) * PITCH for h in range(TH)])
        store_pixels(jnp.where(has_right, hi, 0.0), [(4 + h) * PITCH + 72 for h in range(TH)])

    for copy in fcopies:
        copy.wait_recv()
    halo_pixels()

    g2 = jnp.concatenate([gain2_v[...].reshape(1, CH), jnp.zeros((1, 256 - CH), F32)], axis=1)
    inside = c < CH
    ones_row = (iota((192, KWIN * KWIN), 0) & 31) == HEAD
    tops = {}

    def pixels(ref, half, w, first_row, count_rows, first_col, count_cols):
        return jnp.concatenate(
            [
                ref[half, pl.ds((first_row + p) * PITCH + first_col + w * WIN, count_cols), :]
                for p in range(count_rows)
            ],
            axis=0,
        )

    def project(w):
        keys_in = jnp.concatenate(
            [pixels(npad, half, w, 0, KWIN, 4, KWIN).astype(BF16) for half in range(2)], axis=1
        )
        kwin[w] = mm(keys_in, wk[...]).astype(BF16)
        vwin[w] = jnp.where(ones_row, 1.0, mm_nt(wvt[...], keys_in)).astype(BF16)
        query_in = jnp.concatenate(
            [pixels(npad, half, w, 4, WIN, 8, WIN).astype(BF16) for half in range(2)], axis=1
        )
        qwin[w] = mm_nt(wqt[...], query_in) * QSCALE

    def score(number, w, head):
        mine = (r >= HEAD * head) & (r < HEAD * (head + 1))
        q = jnp.where(mine, qwin[w], 0.0).astype(BF16)
        top = None
        for part in (slice(0, 288), slice(288, 576)):
            scores = mm(kwin[w, part, :], q) + bias[head, part, :]
            sbuf[number % 2, part, :] = scores
            best = jnp.max(scores, axis=0, keepdims=True)
            top = best if top is None else jnp.maximum(top, best)
        tops[number] = top

    def exponent(number):
        pbuf[number % 2] = jnp.exp2(sbuf[number % 2] - tops[number]).astype(BF16)

    def combine(number, w, head):
        rows = slice(SLOT * head, SLOT * (head + 1))
        mixed_values = mm(vwin[w, rows, :], pbuf[number % 2])
        attt[w, rows, :] = (mixed_values / mixed_values[HEAD : HEAD + 1, :]).astype(BF16)

    def feed_forward(w):
        attended = mm_nt(identity, attt[w]).astype(BF16)
        base = jnp.concatenate([pixels(fpad, half, w, 4, WIN, 8, WIN) for half in range(2)], axis=1)
        first = base + mm(attended, pw[0:192, :])
        center = first - jnp.sum(first, axis=-1, keepdims=True) * (1.0 / CH)
        center = jnp.where(inside, center, 0.0)
        spread = jnp.sum(center * center, axis=-1, keepdims=True) * (1.0 / CH)
        second = (center * lax.rsqrt(spread + 1e-05) * g2).astype(BF16)
        inner = mm(second, hpad[...])
        inner = (0.5 * inner * (1.0 + lax.erf(inner * math.sqrt(0.5)))).astype(BF16)
        mixed = first + mm(inner, wout[...])
        for i in range(WIN):
            block = mixed[WIN * i : WIN * (i + 1), :]
            rows = pl.ds((3 + i) * PITCH + 8 + w * WIN, WIN)
            mixpad[0, rows, :] = block[:, 0:128]
            mixpad[1, rows, :] = block[:, 128:256]
            mix_own[i, w * WIN : (w + 1) * WIN, :] = block.astype(BF16)

    mcopies = exchange(
        [
            (mix_own.at[:, 0:16], mix_r, (row, left)),
            (mix_own.at[:, 48:64], mix_l, (row, right)),
            (mix_own.at[0:3, 0:16], mix_c.at[3], (up, left)),
            (mix_own.at[0:3, 48:64], mix_c.at[2], (up, right)),
            (mix_own.at[13:16, 0:16], mix_c.at[1], (down, left)),
            (mix_own.at[13:16, 48:64], mix_c.at[0], (down, right)),
            (mix_own.at[0:3, 0:16], mix_b.at[:, 0:16], (up, col)),
            (mix_own.at[0:3, 48:64], mix_b.at[:, 48:64], (up, col)),
            (mix_own.at[13:16, 0:16], mix_t.at[:, 0:16], (down, col)),
            (mix_own.at[13:16, 48:64], mix_t.at[:, 48:64], (down, col)),
            (mix_own.at[0:3, 16:48], mix_b.at[:, 16:48], (up, col)),
            (mix_own.at[13:16, 16:48], mix_t.at[:, 16:48], (down, col)),
        ],
        msend, mrecv,
    )
    windows = (0, 3, 1, 2)
    steps = [(w, head) for w in windows for head in range(HEADS)]

    def attend(first, last):
        for number in range(first, last + 2):
            if number < last:
                w, head = steps[number]
                if head == 0:
                    project(w)
                score(number, w, head)
            if first <= number - 1 < last:
                exponent(number - 1)
            if first <= number - 2 < last:
                combine(number - 2, *steps[number - 2])
                if number - 2 == first + 5:
                    feed_forward(steps[number - 2][0])
        feed_forward(steps[last - 1][0])

    def edge_windows():
        attend(0, 12)

    def inner_windows():
        attend(12, 24)

    edge_windows()
    for copy in mcopies[0:10]:
        copy.start()
    inner_windows()
    for copy in mcopies[10:12]:
        copy.start()

    def store_mixed(start, count, values, valid):
        x = jnp.where(valid, values, 0.0)
        rows = pl.ds(start, count)
        mixpad[0, rows, :] = x[:, 0:128]
        mixpad[1, rows, :] = x[:, 128:256]

    def side_mixed():
        for h in range(TH):
            start = (3 + h) * PITCH
            store_mixed(start, 8, mix_l[h].astype(F32)[8:16], has_left)
            store_mixed(start + 72, 8, mix_r[h].astype(F32)[0:8], has_right)

    def ends_mixed():
        for h in range(3):
            for ref, first, valid, kinds in ((mix_t, 0, has_up, (0, 1)), (mix_b, 19, has_down, (2, 3))):
                start = (first + h) * PITCH
                store_mixed(start + 8, TW, ref[h].astype(F32), valid)
                store_mixed(start, 8, mix_c[kinds[0], h].astype(F32)[8:16], valid & has_left)
                store_mixed(start + 72, 8, mix_c[kinds[1], h].astype(F32)[0:8], valid & has_right)

    def conv_group(h0, count):
        acc = None
        for a in range(3):
            for b in range(3):
                halves = []
                for half in range(2):
                    rows = [
                        mixpad[half, pl.ds((h0 + k + a) * PITCH + 5 + b, GP), :] for k in range(count)
                    ]
                    halves.append(jnp.concatenate(rows, axis=0).astype(BF16))
                term = mm(jnp.concatenate(halves, axis=1), gpad[3 * a + b])
                acc = term if acc is None else acc + term
        for k in range(count):
            h = h0 + k
            for half in range(2):
                base = fpad[half, pl.ds((h + 2) * PITCH + 6, GP), :]
                value = base + acc[GP * k : GP * (k + 1), 128 * half : 128 * half + 128]
                gbuf[half, pl.ds(h * GP, GP), :] = value

    def group_inner():
        for h0 in range(3, 17, 2):
            conv_group(h0, 2)

    def group_ends():
        for h0 in (0, 17):
            conv_group(h0, 2)
            conv_group(h0 + 2, 1)

    for copy in mcopies[0:2]:
        copy.wait_recv()
    side_mixed()
    group_inner()
    for copy in mcopies[2:12]:
        copy.wait_recv()
    ends_mixed()
    group_ends()

    def clear_rim(ref, lead, count, rim):
        def clear(start, size):
            if lead:
                ref[:, pl.ds(start, size), :] = jnp.zeros((2, size, 128), F32)
            else:
                ref[pl.ds(start, size), :] = jnp.zeros((size, 128), F32)

        @pl.when(jnp.logical_not(has_up))
        def _():
            clear(0, rim * GP)

        @pl.when(jnp.logical_not(has_down))
        def _():
            clear((count - rim) * GP, rim * GP)

        @pl.when(jnp.logical_not(has_left))
        def _():
            for h in range(count):
                clear(h * GP, rim)

        @pl.when(jnp.logical_not(has_right))
        def _():
            for h in range(count):
                clear(h * GP + TW + rim, rim)

    clear_rim(gbuf, True, 20, 2)

    low_lanes = iota((6 * GP, 128), 1) < 64
    low64 = iota((TW, 128), 1) < 64

    def before():
        ybuf[:, 18 * GP :, :] = jnp.zeros((2, 8, 128), F32)
        lbuf[18 * GP :, :] = jnp.zeros((8, 128), F32)
        for step in range(3):
            start = step * (6 * GP)
            acc = None
            for a in range(3):
                rows = pl.ds(start + a * GP, 6 * GP)
                lhs = jnp.concatenate([gbuf[half, rows, :].astype(BF16) for half in range(2)], axis=1)
                term = mm(lhs, w2[a])
                acc = term if acc is None else acc + term
            rows = pl.ds(start, 6 * GP)
            ybuf[0, rows, :] = acc[:, 0:128]
            ybuf[1, rows, :] = acc[:, 128:256]
        for step in range(3):
            start = step * (6 * GP)
            value = (
                ybuf[0, pl.ds(start, 6 * GP), :]
                + pltpu.roll(ybuf[0, pl.ds(start + 1, 6 * GP), :], 64, 1)
                + ybuf[1, pl.ds(start + 2, 6 * GP), :]
            )
            value = jnp.where(value >= 0, value, 0.01 * value)
            lbuf[pl.ds(start, 6 * GP), :] = jnp.where(low_lanes, value, pltpu.roll(value, 64, 1))

    before()
    clear_rim(lbuf, False, 18, 1)

    def gather_taps():
        for h in range(18):
            start = h * GP
            zero = lbuf[pl.ds(start, TW), :]
            one = lbuf[pl.ds(start + 1, TW), :]
            two = lbuf[pl.ds(start + 2, TW), :]
            l3[h, :, 0:128] = jnp.where(low64, zero, one).astype(BF16)
            l3[h, :, 128:256] = jnp.where(low64, two, 0.0).astype(BF16)

    gather_taps()

    target = 128 * (lax.shift_right_logical(r, 6) & 1) + 2 * (r & 63) + lax.shift_right_logical(r, 7)
    weave = one_hot(c == target)

    def conv_up():
        for step in range(4):
            acc = None
            for a in range(3):
                rhs = jnp.concatenate([l3[4 * step + a + k] for k in range(4)], axis=0)
                term = mm_nt(w3[a], rhs)
                acc = term if acc is None else acc + term
            acc = acc.astype(BF16)
            for pair in range(2):
                lanes = slice(128 * pair, 128 * pair + 128)
                both = jnp.concatenate([acc[0:128, lanes], acc[128:256, lanes]], axis=1)
                woven = mm(both, weave)
                for k in range(2):
                    for a in range(2):
                        line = (2 * (4 * step + 2 * pair + k) + a) % 16
                        obuf[step // 2, pl.ds(line, 64, stride=16), :] = woven[
                            64 * a : 64 * (a + 1), 128 * k : 128 * k + 128
                        ]
            if step % 2:
                half = step // 2
                out[:, 16 * half : 16 * half + 16, :] = (
                    obuf[half].reshape(64, 16, 128).astype(BF16)
                )

    conv_up()
    for copy in fcopies + mcopies:
        copy.wait_send()


def on_device(
    nr, nc, features, gain_one, qkv_weight, bias_table, proj_weight, gain_two,
    hidden_weight, output_weight, group_conv, before_conv, upsample_conv,
):
    selector = jnp.asarray(table_selector(), BF16)
    operands = (
        features, gain_one, qkv_weight, bias_table.T, proj_weight, gain_two, hidden_weight,
        output_weight.T, group_conv, before_conv.transpose(0, 1, 3, 2),
        upsample_conv.reshape(3, 192, 256), selector,
    )
    any_space = pl.BlockSpec(memory_space=pltpu.HBM)
    staged = [pltpu.VMEM(x.shape, x.dtype) for x in operands]
    staged[10] = pltpu.VMEM((3, 256, 256), BF16)
    scratch = staged + [
        pltpu.VMEM((4, TW, CH), BF16), pltpu.VMEM((4, TW, CH), BF16),
        pltpu.VMEM((TH, 16, CH), BF16), pltpu.VMEM((TH, 16, CH), BF16),
        pltpu.VMEM((4, 4, 16, CH), BF16),
        pltpu.VMEM((3, TW, 256), BF16), pltpu.VMEM((3, TW, 256), BF16),
        pltpu.VMEM((TH, 16, 256), BF16), pltpu.VMEM((TH, 16, 256), BF16),
        pltpu.VMEM((4, 3, 16, 256), BF16), pltpu.VMEM((TH, TW, 256), BF16),
        pltpu.VMEM((2, 24 * PITCH, 128), F32), pltpu.VMEM((2, 24 * PITCH, 128), F32),
        pltpu.VMEM((2, 22 * PITCH, 128), F32), pltpu.VMEM((2, 20 * GP, 128), F32),
        pltpu.VMEM((2, 18 * GP + 8, 128), F32), pltpu.VMEM((18 * GP + 8, 128), F32),
        pltpu.VMEM((18, TW, 256), BF16),
        pltpu.VMEM((256, 640), BF16), pltpu.VMEM((256, 256), BF16), pltpu.VMEM((256, 256), BF16),
        pltpu.VMEM((192, 256), BF16), pltpu.VMEM((256, 256), BF16), pltpu.VMEM((256, 256), BF16),
        pltpu.VMEM((256, 384), BF16), pltpu.VMEM((256, 384), BF16), pltpu.VMEM((384, 256), BF16),
        pltpu.VMEM((9, 256, 256), BF16), pltpu.VMEM((3, 256, 256), BF16),
        pltpu.VMEM((3, 256, 256), BF16), pltpu.VMEM((3, 256, 256), BF16),
        pltpu.VMEM((HEADS, KWIN * KWIN, 256), F32), pltpu.VMEM((HEADS, KWIN, 640), F32),
        pltpu.VMEM((4, KWIN * KWIN, 256), BF16), pltpu.VMEM((4, 192, KWIN * KWIN), BF16),
        pltpu.VMEM((4, 256, 256), F32), pltpu.VMEM((2, KWIN * KWIN, 256), F32),
        pltpu.VMEM((2, KWIN * KWIN, 256), BF16), pltpu.VMEM((4, 192, 256), BF16),
        pltpu.VMEM((2, 64 * 16, 128), F32),
        pltpu.SemaphoreType.DMA((12,)), pltpu.SemaphoreType.DMA((8,)), pltpu.SemaphoreType.DMA((8,)),
        pltpu.SemaphoreType.DMA((12,)), pltpu.SemaphoreType.DMA((12,)),
    ]
    result = pl.pallas_call(
        functools.partial(kernel, nr, nc),
        out_shape=jax.ShapeDtypeStruct((64, 2 * TH, 2 * TW), BF16),
        in_specs=[any_space] * len(operands),
        out_specs=pl.BlockSpec(memory_space=pltpu.VMEM),
        scratch_shapes=scratch,
        compiler_params=pltpu.CompilerParams(
            collective_id=0, has_side_effects=True, vmem_limit_bytes=62 * 1024 * 1024
        ),
    )(*operands)
    return result


def solution(mesh):
    placed = (P("rows", "cols", None),) + (P(),) * 10
    body = functools.partial(on_device, mesh.shape["rows"], mesh.shape["cols"])
    return jax.shard_map(
        body, mesh=mesh, in_specs=placed, out_specs=P(None, "rows", "cols"), check_vma=False
    )
```

time: 64.1 us -> 35.7 us (0.56)
  Pallas kernels: 51 us -> 33.7 us
  local copies, waits for them, and re-layouts: 12.6 us -> 1.87 us
    pallas_call x1, Pallas kernels: 51 us -> 33.7 us  [on_device(): pl.pallas_call(functools.partial(kernel, nr, nc), out_shape=jax.ShapeDtyp...]
    unnamed x24 -> x1, local copies, waits for them, and re-layouts: 11.5 us -> 1.87 us
    transpose x1 -> x0, local copies, waits for them, and re-layouts: 1.14 us -> none  [on_device(): return result.transpose(1, 0, 2)]
where the time goes in v2:
time: 35.7 us; the launch traced here: 35.6 us
  Pallas kernels  33.7 us (94%)
  local copies, waits for them, and re-layouts  1.87 us (5%)
    pallas_call x1, Pallas kernels, on_device(): pl.pallas_call(functools.partial(kernel, nr, nc), out_shape=jax.ShapeDtyp...  33.7 us
    unnamed x1, local copies, waits for them, and re-layouts  1.87 us

profile of v2, /device:TPU:1, one launch (start us, length us, event | category | flops | bytes accessed | tf_op | source)
XLA Modules:
  0.0 35.6 jit_solution(9731306178927244811)
XLA Ops:
  0.0 33.7 %shard_map.118 = bf16[64,32,128]{2,1,0:T(8,128)(2,1)} custom-call(bf16[16,64,180]{2,1,0:T(8,128)(2,1)} %feat.1, f32[180]{0:T(256)} %gain1.1, bf16[180,540]{1,0:T(8,128)(2,1)} %qkv.1, f32[6,1521]{1,0:T(8,128)} %bitcast.7, bf16[180,180]{1,0:T(8,128)(2,1)} %proj.1, f32[180]{0:T(256)} %gain2.1, bf16[180,360]{1,0:T(8,128)(2,1)} %hid.1, bf16[180,360]{1,0:T(8,128)(2,1)} %bitcast.6, ...), custom_call_target="tpu_custom_call" | custom-call | tf_op jit(solution)/shard_map/pallas_call | solution.py:578
  33.7 1.9 %copy.14 = bf16[64,32,128]{2,1,0:T(8,128)(2,1)} copy(bf16[64,32,128]{2,1,0:T(8,128)(2,1)} %shard_map.118) | data formatting | bytes 1048576

commit v3 on v2

v3 whole, which is shorter than its diff:
```python
import functools
import math

import jax
import jax.numpy as jnp
import numpy as np
from jax import lax
from jax.experimental import pallas as pl
from jax.experimental.pallas import tpu as pltpu
from jax.sharding import PartitionSpec as P

HEADS = 6
HEAD = 30
SLOT = 32
CH = 180
WIN = 16
KWIN = 24
SIDE = WIN + KWIN - 1
TABLE = SIDE * SIDE
TH = 16
TW = 64
PITCH = 80
GP = 72
QSCALE = math.log2(math.e) / math.sqrt(HEAD)
LOG2E = math.log2(math.e)
F32 = jnp.float32
BF16 = jnp.bfloat16
MESH = pl.DeviceIdType.MESH
NT = (((1,), (1,)), ((), ()))


def table_selector():
    out = np.zeros((384, 384), np.float32)
    for lane in range(128):
        for part in range(3):
            entry = 16 * part + lane % 16
            if entry < SIDE:
                out[SIDE * (7 - lane // 16) + SIDE - 1 - entry, 128 * part + lane] = 1.0
    return out


def mm(a, b):
    return jnp.dot(a, b, preferred_element_type=F32)


def mm_nt(a, b):
    return lax.dot_general(a, b, NT, preferred_element_type=F32)


def iota(shape, dim):
    return lax.broadcasted_iota(jnp.int32, shape, dim)


def one_hot(mask):
    return jnp.where(mask, 1.0, 0.0).astype(BF16)


def normalize(x, gain):
    lane = iota(x[1].shape, 1)
    mean = jnp.sum(x[0] + x[1], axis=-1, keepdims=True) * (1.0 / CH)
    low = x[0] - mean
    high = jnp.where(lane < CH - 128, x[1] - mean, 0.0)
    spread = jnp.sum(low * low + high * high, axis=-1, keepdims=True) * (1.0 / CH)
    scale = lax.rsqrt(spread + 1e-05)
    return low * scale * gain[:, 0:128], high * scale * gain[:, 128:256]


def pack_pixels(low, high):
    half = low.shape[0] // 2
    lane = iota((half, 128), 1)
    joined = jnp.where(lane < 64, high[:half], pltpu.roll(high[half:], 64, 1))
    return jnp.concatenate([low, joined], axis=0).astype(BF16)


def unpack_pixels(packed, valid):
    count = packed.shape[0] * 2 // 3
    x = jnp.where(valid, packed.astype(F32), 0.0)
    joined = x[count:]
    high = jnp.concatenate([joined, pltpu.roll(joined, 64, 1)], axis=0)
    return x[:count], jnp.where(iota(high.shape, 1) < CH - 128, high, 0.0)


def kernel(
    nr, nc,
    feat, gain1, qkv, table, proj, gain2, hid, outw, gconv, bconv, uconv, selector,
    out,
    feat_v, gain1_v, qkv_v, table_v, proj_v, gain2_v, hid_v, outw_v, gconv_v, bconv_v, upad, sel_v,
    send_t, send_b, send_l, send_r, send_c, halo_t, halo_b, halo_l, halo_r, halo_c,
    mix_t, mix_b, mix_l, mix_r, mix_c, mix_own,
    fpad, npad, mixpad, gbuf, ybuf, lbuf, l3,
    qpad, wqt, wk, wvt, ppad, pw, hpad, opad, wout, gpad, bpad, w2, w3, bias, xwin, kwin, vwin, qwin, sbuf, pbuf, attt, fbuf, second, inner, obuf,
    local_sem, fsend, frecv, msend, mrecv,
):
    row = lax.axis_index("rows")
    col = lax.axis_index("cols")
    up = lax.rem(row + nr - 1, nr)
    down = lax.rem(row + 1, nr)
    left = lax.rem(col + nc - 1, nc)
    right = lax.rem(col + 1, nc)
    neighbours = [
        (up, col), (down, col), (row, left), (row, right),
        (up, left), (up, right), (down, left), (down, right),
    ]
    barrier = pltpu.get_barrier_semaphore()
    for target in neighbours:
        pl.semaphore_signal(barrier, inc=1, device_id=target, device_id_type=MESH)

    local = {}
    pairs = [
        ("feat", feat, feat_v), ("gain1", gain1, gain1_v), ("table", table, table_v),
        ("selector", selector, sel_v), ("qkv", qkv, qkv_v), ("proj", proj, proj_v),
        ("gain2", gain2, gain2_v), ("hid", hid, hid_v), ("outw", outw, outw_v),
        ("gconv", gconv, gconv_v), ("bconv", bconv, bconv_v), ("uconv", uconv, upad.at[:, 0:192, :]),
    ]
    for number, (name, source, target) in enumerate(pairs):
        local[name] = pltpu.make_async_copy(source, target, local_sem.at[number])
    for name in ("feat", "gain1", "table", "selector"):
        local[name].start()

    def arrive(*names):
        for name in names:
            local[name].wait()

    def exchange(specs, send_sem, recv_sem):
        copies = []
        for number, (source, target, device) in enumerate(specs):
            copies.append(
                pltpu.make_async_remote_copy(
                    src_ref=source, dst_ref=target, send_sem=send_sem.at[number],
                    recv_sem=recv_sem.at[number], device_id=device, device_id_type=MESH,
                )
            )
        return copies

    fcopies = exchange(
        [
            (send_t, halo_b, (up, col)),
            (send_b, halo_t, (down, col)),
            (send_l, halo_r, (row, left)),
            (send_r, halo_l, (row, right)),
            (send_c.at[0], halo_c.at[3], (up, left)),
            (send_c.at[1], halo_c.at[2], (up, right)),
            (send_c.at[2], halo_c.at[1], (down, left)),
            (send_c.at[3], halo_c.at[0], (down, right)),
        ],
        fsend, frecv,
    )

    has_up = row > 0
    has_down = row < nr - 1
    has_left = col > 0
    has_right = col < nc - 1

    fpad[1] = jnp.zeros(fpad.shape[1:], F32)
    arrive("feat", "gain1")
    for h in range(0, TH, 4):
        x = feat_v[h : h + 4].astype(F32).reshape(4 * TW, CH)
        for k in range(4):
            rows = pl.ds((h + k + 4) * PITCH + 8, TW)
            fpad[0, rows, :] = x[k * TW : (k + 1) * TW, 0:128]
            fpad[1, rows, 0 : CH - 128] = x[k * TW : (k + 1) * TW, 128:CH]

    def region(ref, first_row, count_rows, first_col, count_cols):
        return [
            jnp.concatenate(
                [
                    ref[half, pl.ds((first_row + k) * PITCH + first_col, count_cols), :]
                    for k in range(count_rows)
                ],
                axis=0,
            )
            for half in range(2)
        ]

    send_t[...] = pack_pixels(*region(fpad, 4, 4, 8, TW))
    send_b[...] = pack_pixels(*region(fpad, 16, 4, 8, TW))
    send_l[...] = pack_pixels(*region(fpad, 4, TH, 8, 8))
    send_r[...] = pack_pixels(*region(fpad, 4, TH, 64, 8))
    for corner, (first_row, first_col) in enumerate(((4, 8), (4, 64), (16, 8), (16, 64))):
        send_c[corner] = pack_pixels(*region(fpad, first_row, 4, first_col, 8))
    pl.semaphore_wait(barrier, 8)
    for copy in fcopies:
        copy.start()
    for name in ("qkv", "proj", "gain2", "hid", "outw", "gconv", "bconv", "uconv"):
        local[name].start()

    def lanes256(ref):
        return jnp.concatenate([ref[...].reshape(1, CH), jnp.zeros((1, 256 - CH), F32)], axis=1)

    g1 = lanes256(gain1_v)

    def store_normed(x, starts):
        n = normalize(x, g1)
        width = x[0].shape[0] // len(starts)
        for k, start in enumerate(starts):
            for half in range(2):
                npad[half, pl.ds(start, width), :] = n[half][k * width : (k + 1) * width]

    def own_pixels():
        for h in range(0, TH, 4):
            store_normed(
                region(fpad, h + 4, 4, 8, TW), [(h + k + 4) * PITCH + 8 for k in range(4)]
            )

    own_pixels()
    for ref in (qpad, ppad, hpad, opad, gpad, bpad):
        ref[...] = jnp.zeros(ref.shape, ref.dtype)
    for a in range(3):
        upad[a, 192:256, :] = jnp.zeros((64, 256), BF16)

    r = iota((256, 256), 0)
    c = iota((256, 256), 1)
    identity = one_hot(r == c)

    def prepare_bias():
        whole = jnp.concatenate(
            [table_v[...] * LOG2E, jnp.zeros((HEADS, 1536 - TABLE), F32)], axis=1
        )
        whole = jnp.concatenate([whole, jnp.zeros((2, 1536), F32)], axis=0)
        lane8 = iota((8, 128), 1)
        sub8 = iota((8, 128), 0)
        pieces = []
        for tile in range(5):
            first = SIDE * (SIDE - 8 - 8 * tile)
            pieces.append(pltpu.roll(whole, (1536 - first) % 1536, 1)[:, 0:384])
        rows = jnp.concatenate(pieces, axis=0)
        hi = rows.astype(BF16)
        rest = rows - hi.astype(F32)
        mid = rest.astype(BF16)
        low = (rest - mid.astype(F32)).astype(BF16)
        picked = mm(hi, sel_v[...]) + mm(mid, sel_v[...]) + mm(low, sel_v[...])
        lane24 = iota((KWIN, 128), 1)
        for head in range(HEADS):
            tiles = []
            for tile in range(5):
                z = picked[8 * tile + head : 8 * tile + head + 1, :]
                blocks = []
                for part, base in ((1, 7), (0, 15), (0, 7)):
                    first = jnp.broadcast_to(z[:, 128 * part : 128 * part + 128], (8, 128))
                    second = jnp.broadcast_to(z[:, 128 * part + 128 : 128 * part + 256], (8, 128))
                    first = pltpu.roll(first, 128 - base, 1, stride=1, stride_axis=0)
                    second = pltpu.roll(second, 16 - base, 1, stride=1, stride_axis=0)
                    blocks.append(jnp.where((lane8 & 15) + base - sub8 < 16, first, second))
                tiles.append(jnp.concatenate(blocks, axis=0))
            for shift in range(8):
                amount = 16 * shift
                if shift:
                    rolled = [pltpu.roll(t, 128 - amount, 1) for t in tiles]
                    joined = [
                        jnp.where(lane24 < 128 - amount, rolled[k], rolled[k + 1]) for k in range(4)
                    ]
                else:
                    joined = tiles
                for block in range(3):
                    p = KWIN - 1 - 8 * block - shift
                    for half in range(2):
                        bias[head, KWIN * p : KWIN * (p + 1), 128 * half : 128 * half + 128] = (
                            joined[block + half]
                        )

    arrive("table", "selector")
    prepare_bias()

    def prepare_weights():
        qpad[0:CH, 0 : 3 * CH] = qkv_v[...]
        wqt[...] = mm_nt(one_hot((r == c) & (r < CH)), qpad[:, 0:256]).astype(BF16)
        wk[...] = mm(qpad[:, 128:384], one_hot((r == c + 52) & (c < CH))).astype(BF16)
        rv = iota((192, 384), 0)
        cv = iota((192, 384), 1)
        slot_source = HEAD * lax.shift_right_logical(rv, 5) + (rv & 31)
        wvt[...] = mm_nt(one_hot((cv == slot_source + 104) & ((rv & 31) < HEAD)), qpad[:, 256:640]).astype(BF16)
        ppad[0:CH, 0:CH] = proj_v[...]
        slot_source = HEAD * lax.shift_right_logical(r, 5) + (r & 31)
        pw[...] = mm(one_hot((c == slot_source) & ((r & 31) < HEAD) & (r < 192)), ppad[...]).astype(BF16)
        hpad[0:CH, 0 : 2 * CH] = hid_v[...]
        opad[0:CH, 0 : 2 * CH] = outw_v[...]
        wout[...] = mm_nt(one_hot(iota((384, 384), 0) == iota((384, 384), 1)), opad[...]).astype(BF16)
        for tap in range(9):
            gpad[tap, 0:CH, 0:CH] = gconv_v[tap // 3, tap % 3]
        order = 4 * (r & 63) + 2 * (lax.shift_right_logical(r, 6) & 1) + lax.shift_right_logical(r, 7)
        shuffle_rows = one_hot(c == order)
        for a in range(3):
            for b in range(3):
                bpad[a, 64 * b : 64 * (b + 1), 0:CH] = bconv_v[a, b]
            w2[a] = mm_nt(identity, bpad[a]).astype(BF16)
            w3[a] = mm_nt(shuffle_rows, upad[a]).astype(BF16)

    arrive("qkv", "proj", "gain2", "hid", "outw", "gconv", "bconv", "uconv")
    prepare_weights()
    def halo_pixels():
        groups = [
            (halo_t[...], has_up, [h * PITCH + 8 for h in range(4)]),
            (halo_b[...], has_down, [(20 + h) * PITCH + 8 for h in range(4)]),
            (halo_l[...], has_left, [(4 + h) * PITCH for h in range(TH)]),
            (halo_r[...], has_right, [(4 + h) * PITCH + 72 for h in range(TH)]),
            (halo_c[0], has_up & has_left, [h * PITCH for h in range(4)]),
            (halo_c[1], has_up & has_right, [h * PITCH + 72 for h in range(4)]),
            (halo_c[2], has_down & has_left, [(20 + h) * PITCH for h in range(4)]),
            (halo_c[3], has_down & has_right, [(20 + h) * PITCH + 72 for h in range(4)]),
        ]
        for packed, valid, starts in groups:
            x = unpack_pixels(packed, valid)
            width = x[0].shape[0] // len(starts)
            for k, start in enumerate(starts):
                for half in range(2):
                    fpad[half, pl.ds(start, width), :] = x[half][k * width : (k + 1) * width]
            store_normed(x, starts)

    for copy in fcopies:
        copy.wait_recv()
    halo_pixels()

    g2 = lanes256(gain2_v)
    inside = c < CH
    ones_row = (iota((192, KWIN * KWIN), 0) & 31) == HEAD
    tops = {}

    def pixels(ref, half, w, first_row, count_rows, first_col, count_cols):
        return jnp.concatenate(
            [
                ref[half, pl.ds((first_row + p) * PITCH + first_col + w * WIN, count_cols), :]
                for p in range(count_rows)
            ],
            axis=0,
        )

    def project_keys(w):
        keys_in = jnp.concatenate(
            [pixels(npad, half, w, 0, KWIN, 4, KWIN).astype(BF16) for half in range(2)], axis=1
        )
        xwin[...] = keys_in
        kwin[w] = mm(keys_in, wk[...]).astype(BF16)

    def project_values(w):
        vwin[w] = jnp.where(ones_row, 1.0, mm_nt(wvt[...], xwin[...])).astype(BF16)

    def project_queries(w):
        query_in = jnp.concatenate(
            [pixels(npad, half, w, 4, WIN, 8, WIN).astype(BF16) for half in range(2)], axis=1
        )
        qwin[w] = mm_nt(wqt[...], query_in) * QSCALE

    def score(number, w, head):
        mine = (r >= HEAD * head) & (r < HEAD * (head + 1))
        q = jnp.where(mine, qwin[w], 0.0).astype(BF16)
        top = None
        for part in (slice(0, 288), slice(288, 576)):
            scores = mm(kwin[w, part, :], q) + bias[head, part, :]
            sbuf[number % 2, part, :] = scores
            best = jnp.max(scores, axis=0, keepdims=True)
            top = best if top is None else jnp.maximum(top, best)
        tops[number] = top

    def exponent(number):
        pbuf[number % 2] = jnp.exp2(sbuf[number % 2] - tops[number]).astype(BF16)

    def combine(number, w, head):
        rows = slice(SLOT * head, SLOT * (head + 1))
        mixed_values = mm(vwin[w, rows, :], pbuf[number % 2])
        attt[w, rows, :] = (mixed_values / mixed_values[HEAD : HEAD + 1, :]).astype(BF16)

    def merge_heads(w):
        attended = mm_nt(identity, attt[w]).astype(BF16)
        base = jnp.concatenate([pixels(fpad, half, w, 4, WIN, 8, WIN) for half in range(2)], axis=1)
        first = base + mm(attended, pw[0:192, :])
        fbuf[...] = first
        center = first - jnp.sum(first, axis=-1, keepdims=True) * (1.0 / CH)
        center = jnp.where(inside, center, 0.0)
        spread = jnp.sum(center * center, axis=-1, keepdims=True) * (1.0 / CH)
        second[...] = (center * lax.rsqrt(spread + 1e-05) * g2).astype(BF16)

    def hidden(part):
        lanes = slice(128 * part, 128 * part + 128)
        value = mm(second[...], hpad[:, lanes])
        inner[:, lanes] = (0.5 * value * (1.0 + lax.erf(value * math.sqrt(0.5)))).astype(BF16)

    def finish_window(w):
        mixed = fbuf[...] + mm(inner[...], wout[...])
        for i in range(WIN):
            block = mixed[WIN * i : WIN * (i + 1), :]
            rows = pl.ds((3 + i) * PITCH + 8 + w * WIN, WIN)
            mixpad[0, rows, :] = block[:, 0:128]
            mixpad[1, rows, :] = block[:, 128:256]
            mix_own[i, w * WIN : (w + 1) * WIN, :] = block.astype(BF16)
        for copy in mcopies[w]:
            copy.start()

    def strip(w):
        cols = slice(w * WIN, (w + 1) * WIN)
        return [
            (mix_own.at[0:3, cols], mix_b.at[:, cols], (up, col)),
            (mix_own.at[13:16, cols], mix_t.at[:, cols], (down, col)),
        ]

    specs = {
        0: [
            (mix_own.at[:, 0:16], mix_r, (row, left)),
            (mix_own.at[0:3, 0:16], mix_c.at[3], (up, left)),
            (mix_own.at[13:16, 0:16], mix_c.at[1], (down, left)),
        ] + strip(0),
        3: [
            (mix_own.at[:, 48:64], mix_l, (row, right)),
            (mix_own.at[0:3, 48:64], mix_c.at[2], (up, right)),
            (mix_own.at[13:16, 48:64], mix_c.at[0], (down, right)),
        ] + strip(3),
        1: strip(1),
        2: strip(2),
    }
    windows = (0, 3, 1, 2)
    every = exchange([item for w in windows for item in specs[w]], msend, mrecv)
    mcopies = {0: every[0:5], 3: every[5:10], 1: every[10:12], 2: every[12:14]}
    steps = [(w, head) for w in windows for head in range(HEADS)]

    def attend():
        project_keys(0)
        project_values(0)
        project_queries(0)
        for number in range(len(steps) + 2):
            place, head = divmod(number, HEADS)
            if number < len(steps):
                score(number, windows[place], head)
            if 0 <= number - 1 < len(steps):
                exponent(number - 1)
            if 0 <= number - 2:
                combine(number - 2, *steps[number - 2])
            if place + 1 < len(windows) and head < 3:
                (project_keys, project_values, project_queries)[head](windows[place + 1])
            if 0 < place < len(windows):
                if head == 1:
                    merge_heads(windows[place - 1])
                elif 2 <= head <= 4:
                    hidden(head - 2)
                elif head == 5:
                    finish_window(windows[place - 1])
        merge_heads(windows[-1])
        for part in range(3):
            hidden(part)
        finish_window(windows[-1])

    attend()

    def store_mixed(start, count, values, valid):
        x = jnp.where(valid, values, 0.0)
        rows = pl.ds(start, count)
        mixpad[0, rows, :] = x[:, 0:128]
        mixpad[1, rows, :] = x[:, 128:256]

    def side_mixed():
        for h in range(TH):
            start = (3 + h) * PITCH
            store_mixed(start, 8, mix_l[h].astype(F32)[8:16], has_left)
            store_mixed(start + 72, 8, mix_r[h].astype(F32)[0:8], has_right)

    def ends_mixed():
        for h in range(3):
            for ref, first, valid, kinds in ((mix_t, 0, has_up, (0, 1)), (mix_b, 19, has_down, (2, 3))):
                start = (first + h) * PITCH
                store_mixed(start + 8, TW, ref[h].astype(F32), valid)
                store_mixed(start, 8, mix_c[kinds[0], h].astype(F32)[8:16], valid & has_left)
                store_mixed(start + 72, 8, mix_c[kinds[1], h].astype(F32)[0:8], valid & has_right)

    cols72 = iota((GP, 128), 0)
    gcols = ((cols72 >= 2) | has_left) & ((cols72 < 66) | has_right)
    lcols = ((cols72 >= 1) | has_left) & ((cols72 < 65) | has_right)

    def conv_group(h0, count):
        acc = None
        for a in range(3):
            for b in range(3):
                halves = []
                for half in range(2):
                    rows = [
                        mixpad[half, pl.ds((h0 + k + a) * PITCH + 5 + b, GP), :] for k in range(count)
                    ]
                    halves.append(jnp.concatenate(rows, axis=0).astype(BF16))
                term = mm(jnp.concatenate(halves, axis=1), gpad[3 * a + b])
                acc = term if acc is None else acc + term
        for k in range(count):
            h = h0 + k
            keep = gcols & has_up if h < 2 else gcols & has_down if h >= 18 else gcols
            for half in range(2):
                base = fpad[half, pl.ds((h + 2) * PITCH + 6, GP), :]
                value = base + acc[GP * k : GP * (k + 1), 128 * half : 128 * half + 128]
                gbuf[half, pl.ds(h * GP, GP), :] = jnp.where(keep, value, 0.0)

    low_lanes = iota((GP, 128), 1) < 64
    low64 = iota((TW, 128), 1) < 64

    def conv_before(first, count):
        start = first * GP
        acc = None
        for a in range(3):
            rows = pl.ds(start + a * GP, count * GP)
            lhs = jnp.concatenate([gbuf[half, rows, :].astype(BF16) for half in range(2)], axis=1)
            term = mm(lhs, w2[a])
            acc = term if acc is None else acc + term
        rows = pl.ds(start, count * GP)
        ybuf[0, rows, :] = acc[:, 0:128]
        ybuf[1, rows, :] = acc[:, 128:256]
        for h in range(first, first + count):
            start = h * GP
            value = (
                ybuf[0, pl.ds(start, GP), :]
                + pltpu.roll(ybuf[0, pl.ds(start + 1, GP), :], 64, 1)
                + ybuf[1, pl.ds(start + 2, GP), :]
            )
            value = jnp.where(value >= 0, value, 0.01 * value)
            keep = lcols & has_up if h < 1 else lcols & has_down if h >= 17 else lcols
            value = jnp.where(keep, value, 0.0)
            lbuf[pl.ds(start, GP), :] = jnp.where(low_lanes, value, pltpu.roll(value, 64, 1))
        for h in range(first, first + count):
            start = h * GP
            zero = lbuf[pl.ds(start, TW), :]
            one = lbuf[pl.ds(start + 1, TW), :]
            two = lbuf[pl.ds(start + 2, TW), :]
            l3[h, :, 0:128] = jnp.where(low64, zero, one).astype(BF16)
            l3[h, :, 128:256] = jnp.where(low64, two, 0.0).astype(BF16)

    target = 128 * (lax.shift_right_logical(r, 6) & 1) + 2 * (r & 63) + lax.shift_right_logical(r, 7)
    weave = one_hot(c == target)

    def conv_up(step):
        acc = None
        for a in range(3):
            rhs = jnp.concatenate([l3[4 * step + a + k] for k in range(4)], axis=0)
            term = mm_nt(w3[a], rhs)
            acc = term if acc is None else acc + term
        acc = acc.astype(BF16)
        for pair in range(2):
            lanes = slice(128 * pair, 128 * pair + 128)
            both = jnp.concatenate([acc[0:128, lanes], acc[128:256, lanes]], axis=1)
            woven = mm(both, weave)
            for k in range(2):
                for a in range(2):
                    line = (2 * (4 * step + 2 * pair + k) + a) % 16
                    obuf[step // 2, pl.ds(line, 64, stride=16), :] = woven[
                        64 * a : 64 * (a + 1), 128 * k : 128 * k + 128
                    ]

    def inner_rows():
        for h0 in range(3, 17, 2):
            conv_group(h0, 2)
        conv_before(3, 6)
        conv_before(9, 6)
        conv_up(1)
        conv_up(2)

    def end_rows():
        for h0 in (0, 17):
            conv_group(h0, 2)
            conv_group(h0 + 2, 1)
        conv_before(0, 3)
        conv_before(15, 3)
        conv_up(0)
        conv_up(3)
        for half in range(2):
            out[:, 16 * half : 16 * half + 16, :] = obuf[half].reshape(64, 16, 128).astype(BF16)

    ybuf[:, 18 * GP :, :] = jnp.zeros((2, 8, 128), F32)
    for number in (0, 5):
        every[number].wait_recv()
    side_mixed()
    inner_rows()
    for number in (1, 2, 3, 4, 6, 7, 8, 9, 10, 11, 12, 13):
        every[number].wait_recv()
    ends_mixed()
    end_rows()
    for copy in fcopies + every:
        copy.wait_send()


def on_device(
    nr, nc, features, gain_one, qkv_weight, bias_table, proj_weight, gain_two,
    hidden_weight, output_weight, group_conv, before_conv, upsample_conv,
):
    selector = jnp.asarray(table_selector(), BF16)
    operands = (
        features, gain_one, qkv_weight, bias_table.T, proj_weight, gain_two, hidden_weight,
        output_weight.T, group_conv, before_conv.transpose(0, 1, 3, 2),
        upsample_conv.reshape(3, 192, 256), selector,
    )
    any_space = pl.BlockSpec(memory_space=pltpu.HBM)
    staged = [pltpu.VMEM(x.shape, x.dtype) for x in operands]
    staged[10] = pltpu.VMEM((3, 256, 256), BF16)
    scratch = staged + [
        pltpu.VMEM((384, 128), BF16), pltpu.VMEM((384, 128), BF16),
        pltpu.VMEM((192, 128), BF16), pltpu.VMEM((192, 128), BF16), pltpu.VMEM((4, 48, 128), BF16),
        pltpu.VMEM((384, 128), BF16), pltpu.VMEM((384, 128), BF16),
        pltpu.VMEM((192, 128), BF16), pltpu.VMEM((192, 128), BF16), pltpu.VMEM((4, 48, 128), BF16),
        pltpu.VMEM((3, TW, 256), BF16), pltpu.VMEM((3, TW, 256), BF16),
        pltpu.VMEM((TH, 16, 256), BF16), pltpu.VMEM((TH, 16, 256), BF16),
        pltpu.VMEM((4, 3, 16, 256), BF16), pltpu.VMEM((TH, TW, 256), BF16),
        pltpu.VMEM((2, 24 * PITCH, 128), F32), pltpu.VMEM((2, 24 * PITCH, 128), F32),
        pltpu.VMEM((2, 22 * PITCH, 128), F32), pltpu.VMEM((2, 20 * GP, 128), F32),
        pltpu.VMEM((2, 18 * GP + 8, 128), F32), pltpu.VMEM((18 * GP + 8, 128), F32),
        pltpu.VMEM((18, TW, 256), BF16),
        pltpu.VMEM((256, 640), BF16), pltpu.VMEM((256, 256), BF16), pltpu.VMEM((256, 256), BF16),
        pltpu.VMEM((192, 256), BF16), pltpu.VMEM((256, 256), BF16), pltpu.VMEM((256, 256), BF16),
        pltpu.VMEM((256, 384), BF16), pltpu.VMEM((256, 384), BF16), pltpu.VMEM((384, 256), BF16),
        pltpu.VMEM((9, 256, 256), BF16), pltpu.VMEM((3, 256, 256), BF16),
        pltpu.VMEM((3, 256, 256), BF16), pltpu.VMEM((3, 256, 256), BF16),
        pltpu.VMEM((HEADS, KWIN * KWIN, 256), F32), pltpu.VMEM((KWIN * KWIN, 256), BF16),
        pltpu.VMEM((4, KWIN * KWIN, 256), BF16), pltpu.VMEM((4, 192, KWIN * KWIN), BF16),
        pltpu.VMEM((4, 256, 256), F32), pltpu.VMEM((2, KWIN * KWIN, 256), F32),
        pltpu.VMEM((2, KWIN * KWIN, 256), BF16), pltpu.VMEM((4, 192, 256), BF16),
        pltpu.VMEM((256, 256), F32), pltpu.VMEM((256, 256), BF16), pltpu.VMEM((256, 384), BF16),
        pltpu.VMEM((2, 64 * 16, 128), F32),
        pltpu.SemaphoreType.DMA((12,)), pltpu.SemaphoreType.DMA((8,)), pltpu.SemaphoreType.DMA((8,)),
        pltpu.SemaphoreType.DMA((14,)), pltpu.SemaphoreType.DMA((14,)),
    ]
    result = pl.pallas_call(
        functools.partial(kernel, nr, nc),
        out_shape=jax.ShapeDtypeStruct((64, 2 * TH, 2 * TW), BF16),
        in_specs=[any_space] * len(operands),
        out_specs=pl.BlockSpec(memory_space=pltpu.VMEM),
        scratch_shapes=scratch,
        compiler_params=pltpu.CompilerParams(
            collective_id=0, has_side_effects=True, vmem_limit_bytes=62 * 1024 * 1024
        ),
    )(*operands)
    return result


def solution(mesh):
    placed = (P("rows", "cols", None),) + (P(),) * 10
    body = functools.partial(on_device, mesh.shape["rows"], mesh.shape["cols"])
    return jax.shard_map(
        body, mesh=mesh, in_specs=placed, out_specs=P(None, "rows", "cols"), check_vma=False
    )
```

time: 35.7 us -> 31.8 us (0.89)
  the two profiles are of different devices: /device:TPU:1 before, /device:TPU:0 now
where the time goes in v3:
time: 31.8 us; the launch traced here: 31.6 us
  Pallas kernels  29.7 us (93%)
  local copies, waits for them, and re-layouts  1.87 us (6%)
    pallas_call x1, Pallas kernels, on_device(): pl.pallas_call(functools.partial(kernel, nr, nc), out_shape=jax.ShapeDtyp...  29.7 us
    unnamed x1, local copies, waits for them, and re-layouts  1.87 us

profile of v3, /device:TPU:0, one launch (start us, length us, event | category | flops | bytes accessed | tf_op | source)
XLA Modules:
  0.0 31.6 jit_solution(10951643824624342317)
XLA Ops:
  0.0 29.7 %shard_map.118 = bf16[64,32,128]{2,1,0:T(8,128)(2,1)} custom-call(bf16[16,64,180]{2,1,0:T(8,128)(2,1)} %feat.1, f32[180]{0:T(256)} %gain1.1, bf16[180,540]{1,0:T(8,128)(2,1)} %qkv.1, f32[6,1521]{1,0:T(8,128)} %bitcast.7, bf16[180,180]{1,0:T(8,128)(2,1)} %proj.1, f32[180]{0:T(256)} %gain2.1, bf16[180,360]{1,0:T(8,128)(2,1)} %hid.1, bf16[180,360]{1,0:T(8,128)(2,1)} %bitcast.6, ...), custom_call_target="tpu_custom_call" | custom-call | tf_op jit(solution)/shard_map/pallas_call | solution.py:611
  29.7 1.9 %copy.14 = bf16[64,32,128]{2,1,0:T(8,128)(2,1)} copy(bf16[64,32,128]{2,1,0:T(8,128)(2,1)} %shard_map.118) | data formatting | bytes 1048576

commit v4 on v3

--- a/solution.py
+++ b/solution.py
@@ -86,9 +86,9 @@
     out,
     feat_v, gain1_v, qkv_v, table_v, proj_v, gain2_v, hid_v, outw_v, gconv_v, bconv_v, upad, sel_v,
     send_t, send_b, send_l, send_r, send_c, halo_t, halo_b, halo_l, halo_r, halo_c,
-    mix_t, mix_b, mix_l, mix_r, mix_c, mix_own,
+    mix_t, mix_b, mix_l, mix_r, mix_c, mix_sl, mix_sr, mix_sc, mix_own,
     fpad, npad, mixpad, gbuf, ybuf, lbuf, l3,
-    qpad, wqt, wk, wvt, ppad, pw, hpad, opad, wout, gpad, bpad, w2, w3, bias, xwin, kwin, vwin, qwin, sbuf, pbuf, attt, fbuf, second, inner, obuf,
+    qpad, wqt, wk, wvt, ppad, pw, hpad, opad, wout, gpad, bpad, w2, w3, bias, xwin, kwin, vwin, qwin, sbuf, pbuf, attt, fbuf, second, inner, obuf, ostage, osem,
     local_sem, fsend, frecv, msend, mrecv,
 ):
     row = lax.axis_index("rows")
@@ -134,14 +134,16 @@
 
     fcopies = exchange(
         [
-            (send_t, halo_b, (up, col)),
-            (send_b, halo_t, (down, col)),
-            (send_l, halo_r, (row, left)),
+            (send_c.at[3], halo_c.at[0], (down, right)),
+            (send_c.at[1], halo_c.at[2], (up, right)),
+            (send_t.at[0], halo_b.at[0], (up, col)),
+            (send_b.at[0], halo_t.at[0], (down, col)),
             (send_r, halo_l, (row, right)),
             (send_c.at[0], halo_c.at[3], (up, left)),
-            (send_c.at[1], halo_c.at[2], (up, right)),
             (send_c.at[2], halo_c.at[1], (down, left)),
-            (send_c.at[3], halo_c.at[0], (down, right)),
+            (send_l, halo_r, (row, left)),
+            (send_t.at[1], halo_b.at[1], (up, col)),
+            (send_b.at[1], halo_t.at[1], (down, col)),
         ],
         fsend, frecv,
     )
@@ -172,8 +174,9 @@
             for half in range(2)
         ]
 
-    send_t[...] = pack_pixels(*region(fpad, 4, 4, 8, TW))
-    send_b[...] = pack_pixels(*region(fpad, 16, 4, 8, TW))
+    for part in range(2):
+        send_t[part] = pack_pixels(*region(fpad, 4, 4, 8 + 32 * part, 32))
+        send_b[part] = pack_pixels(*region(fpad, 16, 4, 8 + 32 * part, 32))
     send_l[...] = pack_pixels(*region(fpad, 4, TH, 8, 8))
     send_r[...] = pack_pixels(*region(fpad, 4, TH, 64, 8))
     for corner, (first_row, first_col) in enumerate(((4, 8), (4, 64), (16, 8), (16, 64))):
@@ -287,16 +290,14 @@
 
     arrive("qkv", "proj", "gain2", "hid", "outw", "gconv", "bconv", "uconv")
     prepare_weights()
-    def halo_pixels():
+    def halo_pixels(part):
+        side, rim, has_side = ((halo_l, 0, has_left), (halo_r, 72, has_right))[part]
         groups = [
-            (halo_t[...], has_up, [h * PITCH + 8 for h in range(4)]),
-            (halo_b[...], has_down, [(20 + h) * PITCH + 8 for h in range(4)]),
-            (halo_l[...], has_left, [(4 + h) * PITCH for h in range(TH)]),
-            (halo_r[...], has_right, [(4 + h) * PITCH + 72 for h in range(TH)]),
-            (halo_c[0], has_up & has_left, [h * PITCH for h in range(4)]),
-            (halo_c[1], has_up & has_right, [h * PITCH + 72 for h in range(4)]),
-            (halo_c[2], has_down & has_left, [(20 + h) * PITCH for h in range(4)]),
-            (halo_c[3], has_down & has_right, [(20 + h) * PITCH + 72 for h in range(4)]),
+            (halo_t[part], has_up, [h * PITCH + 8 + 32 * part for h in range(4)]),
+            (halo_b[part], has_down, [(20 + h) * PITCH + 8 + 32 * part for h in range(4)]),
+            (side[...], has_side, [(4 + h) * PITCH + rim for h in range(TH)]),
+            (halo_c[part], has_up & has_side, [h * PITCH + rim for h in range(4)]),
+            (halo_c[2 + part], has_down & has_side, [(20 + h) * PITCH + rim for h in range(4)]),
         ]
         for packed, valid, starts in groups:
             x = unpack_pixels(packed, valid)
@@ -305,10 +306,6 @@
                 for half in range(2):
                     fpad[half, pl.ds(start, width), :] = x[half][k * width : (k + 1) * width]
             store_normed(x, starts)
-
-    for copy in fcopies:
-        copy.wait_recv()
-    halo_pixels()
 
     g2 = lanes256(gain2_v)
     inside = c < CH
@@ -382,6 +379,14 @@
             mixpad[0, rows, :] = block[:, 0:128]
             mixpad[1, rows, :] = block[:, 128:256]
             mix_own[i, w * WIN : (w + 1) * WIN, :] = block.astype(BF16)
+        if w == 0:
+            mix_sl[...] = pack_pixels(*region(mixpad, 3, TH, 8, 8))
+            mix_sc[0] = pack_pixels(*region(mixpad, 3, 4, 8, 8))
+            mix_sc[2] = pack_pixels(*region(mixpad, 15, 4, 8, 8))
+        if w == 3:
+            mix_sr[...] = pack_pixels(*region(mixpad, 3, TH, 64, 8))
+            mix_sc[1] = pack_pixels(*region(mixpad, 3, 4, 64, 8))
+            mix_sc[3] = pack_pixels(*region(mixpad, 15, 4, 64, 8))
         for copy in mcopies[w]:
             copy.start()
 
@@ -394,14 +399,14 @@
 
     specs = {
         0: [
-            (mix_own.at[:, 0:16], mix_r, (row, left)),
-            (mix_own.at[0:3, 0:16], mix_c.at[3], (up, left)),
-            (mix_own.at[13:16, 0:16], mix_c.at[1], (down, left)),
+            (mix_sl, mix_r, (row, left)),
+            (mix_sc.at[0], mix_c.at[3], (up, left)),
+            (mix_sc.at[2], mix_c.at[1], (down, left)),
         ] + strip(0),
         3: [
-            (mix_own.at[:, 48:64], mix_l, (row, right)),
-            (mix_own.at[0:3, 48:64], mix_c.at[2], (up, right)),
-            (mix_own.at[13:16, 48:64], mix_c.at[0], (down, right)),
+            (mix_sr, mix_l, (row, right)),
+            (mix_sc.at[1], mix_c.at[2], (up, right)),
+            (mix_sc.at[3], mix_c.at[0], (down, right)),
         ] + strip(3),
         1: strip(1),
         2: strip(2),
@@ -411,11 +416,22 @@
     mcopies = {0: every[0:5], 3: every[5:10], 1: every[10:12], 2: every[12:14]}
     steps = [(w, head) for w in windows for head in range(HEADS)]
 
-    def attend():
+    def first_half():
+        halo_pixels(0)
         project_keys(0)
         project_values(0)
-        project_queries(0)
-        for number in range(len(steps) + 2):
+        attend(0, 3)
+
+    def second_half():
+        halo_pixels(1)
+        attend(3, len(steps) + 2)
+        merge_heads(windows[-1])
+        for part in range(3):
+            hidden(part)
+        finish_window(windows[-1])
+
+    def attend(begin, end):
+        for number in range(begin, end):
             place, head = divmod(number, HEADS)
             if number < len(steps):
                 score(number, windows[place], head)
@@ -423,8 +439,8 @@
                 exponent(number - 1)
             if 0 <= number - 2:
                 combine(number - 2, *steps[number - 2])
-            if place + 1 < len(windows) and head < 3:
-                (project_keys, project_values, project_queries)[head](windows[place + 1])
+            if place + 1 < len(windows) and 3 <= head <= 4:
+                (project_keys, project_values)[head - 3](windows[place + 1])
             if 0 < place < len(windows):
                 if head == 1:
                     merge_heads(windows[place - 1])
@@ -432,12 +448,18 @@
                     hidden(head - 2)
                 elif head == 5:
                     finish_window(windows[place - 1])
-        merge_heads(windows[-1])
-        for part in range(3):
-            hidden(part)
-        finish_window(windows[-1])
-
-    attend()
+
+    def all_queries():
+        for w in windows:
+            project_queries(w)
+
+    all_queries()
+    for number in (0, 1, 2, 3, 4):
+        fcopies[number].wait_recv()
+    first_half()
+    for number in (5, 6, 7, 8, 9):
+        fcopies[number].wait_recv()
+    second_half()
 
     def store_mixed(start, count, values, valid):
         x = jnp.where(valid, values, 0.0)
@@ -445,19 +467,28 @@
         mixpad[0, rows, :] = x[:, 0:128]
         mixpad[1, rows, :] = x[:, 128:256]
 
+    def store_packed(packed, valid, starts, skip=0):
+        x = unpack_pixels(packed, valid)
+        for k, start in enumerate(starts):
+            part = slice((k + skip) * 8, (k + skip + 1) * 8)
+            for half in range(2):
+                mixpad[half, pl.ds(start, 8), :] = x[half][part]
+
     def side_mixed():
-        for h in range(TH):
-            start = (3 + h) * PITCH
-            store_mixed(start, 8, mix_l[h].astype(F32)[8:16], has_left)
-            store_mixed(start + 72, 8, mix_r[h].astype(F32)[0:8], has_right)
-
-    def ends_mixed():
+        store_packed(mix_l[...], has_left, [(3 + h) * PITCH for h in range(TH)])
+        store_packed(mix_r[...], has_right, [(3 + h) * PITCH + 72 for h in range(TH)])
+
+    def top_mixed():
         for h in range(3):
-            for ref, first, valid, kinds in ((mix_t, 0, has_up, (0, 1)), (mix_b, 19, has_down, (2, 3))):
-                start = (first + h) * PITCH
-                store_mixed(start + 8, TW, ref[h].astype(F32), valid)
-                store_mixed(start, 8, mix_c[kinds[0], h].astype(F32)[8:16], valid & has_left)
-                store_mixed(start + 72, 8, mix_c[kinds[1], h].astype(F32)[0:8], valid & has_right)
+            store_mixed(h * PITCH + 8, TW, mix_t[h].astype(F32), has_up)
+        store_packed(mix_c[0], has_up & has_left, [h * PITCH for h in range(3)], 1)
+        store_packed(mix_c[1], has_up & has_right, [h * PITCH + 72 for h in range(3)], 1)
+
+    def bottom_mixed():
+        for h in range(3):
+            store_mixed((19 + h) * PITCH + 8, TW, mix_b[h].astype(F32), has_down)
+        store_packed(mix_c[2], has_down & has_left, [(19 + h) * PITCH for h in range(3)])
+        store_packed(mix_c[3], has_down & has_right, [(19 + h) * PITCH + 72 for h in range(3)])
 
     cols72 = iota((GP, 128), 0)
     gcols = ((cols72 >= 2) | has_left) & ((cols72 < 66) | has_right)
@@ -545,26 +576,44 @@
         conv_up(1)
         conv_up(2)
 
-    def end_rows():
-        for h0 in (0, 17):
-            conv_group(h0, 2)
-            conv_group(h0 + 2, 1)
+    def out_half(half):
+        ostage[half] = obuf[half].reshape(64, 16, 128).astype(BF16)
+
+    def top_rows():
+        conv_group(0, 2)
+        conv_group(2, 1)
         conv_before(0, 3)
+        conv_up(0)
+        out_half(0)
+
+    def bottom_rows():
+        conv_group(17, 2)
+        conv_group(19, 1)
         conv_before(15, 3)
-        conv_up(0)
         conv_up(3)
-        for half in range(2):
-            out[:, 16 * half : 16 * half + 16, :] = obuf[half].reshape(64, 16, 128).astype(BF16)
+        out_half(1)
 
     ybuf[:, 18 * GP :, :] = jnp.zeros((2, 8, 128), F32)
     for number in (0, 5):
         every[number].wait_recv()
     side_mixed()
     inner_rows()
-    for number in (1, 2, 3, 4, 6, 7, 8, 9, 10, 11, 12, 13):
+    stores = [
+        pltpu.make_async_copy(ostage.at[half], out.at[:, 16 * half : 16 * half + 16], osem.at[half])
+        for half in range(2)
+    ]
+    for number in (2, 4, 7, 9, 11, 13):
         every[number].wait_recv()
-    ends_mixed()
-    end_rows()
+    top_mixed()
+    top_rows()
+    stores[0].start()
+    for number in (1, 3, 6, 8, 10, 12):
+        every[number].wait_recv()
+    bottom_mixed()
+    bottom_rows()
+    stores[1].start()
+    for store in stores:
+        store.wait()
     for copy in fcopies + every:
         copy.wait_send()
 
@@ -579,17 +628,18 @@
         output_weight.T, group_conv, before_conv.transpose(0, 1, 3, 2),
         upsample_conv.reshape(3, 192, 256), selector,
     )
-    any_space = pl.BlockSpec(memory_space=pltpu.HBM)
+    any_space = pl.BlockSpec(memory_space=pl.ANY)
     staged = [pltpu.VMEM(x.shape, x.dtype) for x in operands]
     staged[10] = pltpu.VMEM((3, 256, 256), BF16)
     scratch = staged + [
-        pltpu.VMEM((384, 128), BF16), pltpu.VMEM((384, 128), BF16),
+        pltpu.VMEM((2, 192, 128), BF16), pltpu.VMEM((2, 192, 128), BF16),
         pltpu.VMEM((192, 128), BF16), pltpu.VMEM((192, 128), BF16), pltpu.VMEM((4, 48, 128), BF16),
-        pltpu.VMEM((384, 128), BF16), pltpu.VMEM((384, 128), BF16),
+        pltpu.VMEM((2, 192, 128), BF16), pltpu.VMEM((2, 192, 128), BF16),
         pltpu.VMEM((192, 128), BF16), pltpu.VMEM((192, 128), BF16), pltpu.VMEM((4, 48, 128), BF16),
         pltpu.VMEM((3, TW, 256), BF16), pltpu.VMEM((3, TW, 256), BF16),
-        pltpu.VMEM((TH, 16, 256), BF16), pltpu.VMEM((TH, 16, 256), BF16),
-        pltpu.VMEM((4, 3, 16, 256), BF16), pltpu.VMEM((TH, TW, 256), BF16),
+        pltpu.VMEM((192, 128), BF16), pltpu.VMEM((192, 128), BF16), pltpu.VMEM((4, 48, 128), BF16),
+        pltpu.VMEM((192, 128), BF16), pltpu.VMEM((192, 128), BF16), pltpu.VMEM((4, 48, 128), BF16),
+        pltpu.VMEM((TH, TW, 256), BF16),
         pltpu.VMEM((2, 24 * PITCH, 128), F32), pltpu.VMEM((2, 24 * PITCH, 128), F32),
         pltpu.VMEM((2, 22 * PITCH, 128), F32), pltpu.VMEM((2, 20 * GP, 128), F32),
         pltpu.VMEM((2, 18 * GP + 8, 128), F32), pltpu.VMEM((18 * GP + 8, 128), F32),
@@ -604,15 +654,16 @@
         pltpu.VMEM((4, 256, 256), F32), pltpu.VMEM((2, KWIN * KWIN, 256), F32),
         pltpu.VMEM((2, KWIN * KWIN, 256), BF16), pltpu.VMEM((4, 192, 256), BF16),
         pltpu.VMEM((256, 256), F32), pltpu.VMEM((256, 256), BF16), pltpu.VMEM((256, 384), BF16),
-        pltpu.VMEM((2, 64 * 16, 128), F32),
-        pltpu.SemaphoreType.DMA((12,)), pltpu.SemaphoreType.DMA((8,)), pltpu.SemaphoreType.DMA((8,)),
+        pltpu.VMEM((2, 64 * 16, 128), F32), pltpu.VMEM((2, 64, 16, 128), BF16),
+        pltpu.SemaphoreType.DMA((2,)),
+        pltpu.SemaphoreType.DMA((12,)), pltpu.SemaphoreType.DMA((10,)), pltpu.SemaphoreType.DMA((10,)),
         pltpu.SemaphoreType.DMA((14,)), pltpu.SemaphoreType.DMA((14,)),
     ]
     result = pl.pallas_call(
         functools.partial(kernel, nr, nc),
         out_shape=jax.ShapeDtypeStruct((64, 2 * TH, 2 * TW), BF16),
         in_specs=[any_space] * len(operands),
-        out_specs=pl.BlockSpec(memory_space=pltpu.VMEM),
+        out_specs=pl.BlockSpec(memory_space=pl.ANY),
         scratch_shapes=scratch,
         compiler_params=pltpu.CompilerParams(
             collective_id=0, has_side_effects=True, vmem_limit_bytes=62 * 1024 * 1024

time: 31.8 us -> 31.8 us (level)
  no operation moved by 1% of the time
where the time goes in v4:
time: 31.8 us; the launch traced here: 31.6 us
  Pallas kernels  29.7 us (93%)
  local copies, waits for them, and re-layouts  1.87 us (6%)
    pallas_call x1, Pallas kernels, on_device(): pl.pallas_call(functools.partial(kernel, nr, nc), out_shape=jax.ShapeDtyp...  29.7 us
    unnamed x1, local copies, waits for them, and re-layouts  1.87 us

profile of v4, /device:TPU:0, one launch (start us, length us, event | category | flops | bytes accessed | tf_op | source)
XLA Modules:
  0.0 31.6 jit_solution(2744198672358242559)
XLA Ops:
  0.0 29.7 %shard_map.118 = bf16[64,32,128]{2,1,0:T(8,128)(2,1)} custom-call(bf16[16,64,180]{2,1,0:T(8,128)(2,1)} %feat.1, f32[180]{0:T(256)} %gain1.1, bf16[180,540]{1,0:T(8,128)(2,1)} %qkv.1, f32[6,1521]{1,0:T(8,128)} %bitcast.7, bf16[180,180]{1,0:T(8,128)(2,1)} %proj.1, f32[180]{0:T(256)} %gain2.1, bf16[180,360]{1,0:T(8,128)(2,1)} %hid.1, bf16[180,360]{1,0:T(8,128)(2,1)} %bitcast.6, ...), custom_call_target="tpu_custom_call" | custom-call | tf_op jit(solution)/shard_map/pallas_call | solution.py:662
  29.7 1.9 %copy.14 = bf16[64,32,128]{2,1,0:T(8,128)(2,1)} copy(bf16[64,32,128]{2,1,0:T(8,128)(2,1)} %shard_map.118) | data formatting | bytes 1048576

commit v5 on v4

--- a/solution.py
+++ b/solution.py
@@ -97,13 +97,25 @@
     down = lax.rem(row + 1, nr)
     left = lax.rem(col + nc - 1, nc)
     right = lax.rem(col + 1, nc)
-    neighbours = [
-        (up, col), (down, col), (row, left), (row, right),
-        (up, left), (up, right), (down, left), (down, right),
-    ]
+    has_up = row > 0
+    has_down = row < nr - 1
+    has_left = col > 0
+    has_right = col < nc - 1
+    place = {
+        "u": ((up, col), has_up), "d": ((down, col), has_down),
+        "l": ((row, left), has_left), "r": ((row, right), has_right),
+        "ul": ((up, left), has_up & has_left), "ur": ((up, right), has_up & has_right),
+        "dl": ((down, left), has_down & has_left), "dr": ((down, right), has_down & has_right),
+    }
+    opposite = {"u": "d", "d": "u", "l": "r", "r": "l", "ul": "dr", "dr": "ul", "ur": "dl", "dl": "ur"}
     barrier = pltpu.get_barrier_semaphore()
-    for target in neighbours:
-        pl.semaphore_signal(barrier, inc=1, device_id=target, device_id_type=MESH)
+    expected = 0
+    for device, exists in place.values():
+        expected = expected + jnp.where(exists, 1, 0)
+
+        @pl.when(exists)
+        def _(device=device):
+            pl.semaphore_signal(barrier, inc=1, device_id=device, device_id_type=MESH)
 
     local = {}
     pairs = [
@@ -123,35 +135,41 @@
 
     def exchange(specs, send_sem, recv_sem):
         copies = []
-        for number, (source, target, device) in enumerate(specs):
-            copies.append(
-                pltpu.make_async_remote_copy(
-                    src_ref=source, dst_ref=target, send_sem=send_sem.at[number],
-                    recv_sem=recv_sem.at[number], device_id=device, device_id_type=MESH,
-                )
+        for number, (source, target, way) in enumerate(specs):
+            copy = pltpu.make_async_remote_copy(
+                src_ref=source, dst_ref=target, send_sem=send_sem.at[number],
+                recv_sem=recv_sem.at[number], device_id=place[way][0], device_id_type=MESH,
             )
+            copies.append((copy, place[way][1], place[opposite[way]][1]))
         return copies
+
+    def start(copies):
+        for copy, sends, _ in copies:
+            pl.when(sends)(copy.start)
+
+    def wait_recv(copies):
+        for copy, _, receives in copies:
+            pl.when(receives)(copy.wait_recv)
+
+    def wait_send(copies):
+        for copy, sends, _ in copies:
+            pl.when(sends)(copy.wait_send)
 
     fcopies = exchange(
         [
-            (send_c.at[3], halo_c.at[0], (down, right)),
-            (send_c.at[1], halo_c.at[2], (up, right)),
-            (send_t.at[0], halo_b.at[0], (up, col)),
-            (send_b.at[0], halo_t.at[0], (down, col)),
-            (send_r, halo_l, (row, right)),
-            (send_c.at[0], halo_c.at[3], (up, left)),
-            (send_c.at[2], halo_c.at[1], (down, left)),
-            (send_l, halo_r, (row, left)),
-            (send_t.at[1], halo_b.at[1], (up, col)),
-            (send_b.at[1], halo_t.at[1], (down, col)),
+            (send_c.at[3], halo_c.at[0], "dr"),
+            (send_c.at[1], halo_c.at[2], "ur"),
+            (send_t.at[0], halo_b.at[0], "u"),
+            (send_b.at[0], halo_t.at[0], "d"),
+            (send_r, halo_l, "r"),
+            (send_c.at[0], halo_c.at[3], "ul"),
+            (send_c.at[2], halo_c.at[1], "dl"),
+            (send_l, halo_r, "l"),
+            (send_t.at[1], halo_b.at[1], "u"),
+            (send_b.at[1], halo_t.at[1], "d"),
         ],
         fsend, frecv,
     )
-
-    has_up = row > 0
-    has_down = row < nr - 1
-    has_left = col > 0
-    has_right = col < nc - 1
 
     fpad[1] = jnp.zeros(fpad.shape[1:], F32)
     arrive("feat", "gain1")
@@ -181,9 +199,8 @@
     send_r[...] = pack_pixels(*region(fpad, 4, TH, 64, 8))
     for corner, (first_row, first_col) in enumerate(((4, 8), (4, 64), (16, 8), (16, 64))):
         send_c[corner] = pack_pixels(*region(fpad, first_row, 4, first_col, 8))
-    pl.semaphore_wait(barrier, 8)
-    for copy in fcopies:
-        copy.start()
+    pl.semaphore_wait(barrier, expected)
+    start(fcopies)
     for name in ("qkv", "proj", "gain2", "hid", "outw", "gconv", "bconv", "uconv"):
         local[name].start()
 
@@ -387,26 +404,25 @@
             mix_sr[...] = pack_pixels(*region(mixpad, 3, TH, 64, 8))
             mix_sc[1] = pack_pixels(*region(mixpad, 3, 4, 64, 8))
             mix_sc[3] = pack_pixels(*region(mixpad, 15, 4, 64, 8))
-        for copy in mcopies[w]:
-            copy.start()
+        start(mcopies[w])
 
     def strip(w):
         cols = slice(w * WIN, (w + 1) * WIN)
         return [
-            (mix_own.at[0:3, cols], mix_b.at[:, cols], (up, col)),
-            (mix_own.at[13:16, cols], mix_t.at[:, cols], (down, col)),
+            (mix_own.at[0:3, cols], mix_b.at[:, cols], "u"),
+            (mix_own.at[13:16, cols], mix_t.at[:, cols], "d"),
         ]
 
     specs = {
         0: [
-            (mix_sl, mix_r, (row, left)),
-            (mix_sc.at[0], mix_c.at[3], (up, left)),
-            (mix_sc.at[2], mix_c.at[1], (down, left)),
+            (mix_sl, mix_r, "l"),
+            (mix_sc.at[0], mix_c.at[3], "ul"),
+            (mix_sc.at[2], mix_c.at[1], "dl"),
         ] + strip(0),
         3: [
-            (mix_sr, mix_l, (row, right)),
-            (mix_sc.at[1], mix_c.at[2], (up, right)),
-            (mix_sc.at[3], mix_c.at[0], (down, right)),
+            (mix_sr, mix_l, "r"),
+            (mix_sc.at[1], mix_c.at[2], "ur"),
+            (mix_sc.at[3], mix_c.at[0], "dr"),
         ] + strip(3),
         1: strip(1),
         2: strip(2),
@@ -432,33 +448,31 @@
 
     def attend(begin, end):
         for number in range(begin, end):
-            place, head = divmod(number, HEADS)
+            turn, head = divmod(number, HEADS)
             if number < len(steps):
-                score(number, windows[place], head)
+                score(number, windows[turn], head)
             if 0 <= number - 1 < len(steps):
                 exponent(number - 1)
             if 0 <= number - 2:
                 combine(number - 2, *steps[number - 2])
-            if place + 1 < len(windows) and 3 <= head <= 4:
-                (project_keys, project_values)[head - 3](windows[place + 1])
-            if 0 < place < len(windows):
+            if turn + 1 < len(windows) and 3 <= head <= 4:
+                (project_keys, project_values)[head - 3](windows[turn + 1])
+            if 0 < turn < len(windows):
                 if head == 1:
-                    merge_heads(windows[place - 1])
+                    merge_heads(windows[turn - 1])
                 elif 2 <= head <= 4:
                     hidden(head - 2)
                 elif head == 5:
-                    finish_window(windows[place - 1])
+                    finish_window(windows[turn - 1])
 
     def all_queries():
         for w in windows:
             project_queries(w)
 
     all_queries()
-    for number in (0, 1, 2, 3, 4):
-        fcopies[number].wait_recv()
+    wait_recv(fcopies[k] for k in (0, 1, 2, 3, 4))
     first_half()
-    for number in (5, 6, 7, 8, 9):
-        fcopies[number].wait_recv()
+    wait_recv(fcopies[k] for k in (5, 6, 7, 8, 9))
     second_half()
 
     def store_mixed(start, count, values, valid):
@@ -594,28 +608,24 @@
         out_half(1)
 
     ybuf[:, 18 * GP :, :] = jnp.zeros((2, 8, 128), F32)
-    for number in (0, 5):
-        every[number].wait_recv()
+    wait_recv(every[k] for k in (0, 5))
     side_mixed()
     inner_rows()
     stores = [
         pltpu.make_async_copy(ostage.at[half], out.at[:, 16 * half : 16 * half + 16], osem.at[half])
         for half in range(2)
     ]
-    for number in (2, 4, 7, 9, 11, 13):
-        every[number].wait_recv()
+    wait_recv(every[k] for k in (2, 4, 7, 9, 11, 13))
     top_mixed()
     top_rows()
     stores[0].start()
-    for number in (1, 3, 6, 8, 10, 12):
-        every[number].wait_recv()
+    wait_recv(every[k] for k in (1, 3, 6, 8, 10, 12))
     bottom_mixed()
     bottom_rows()
     stores[1].start()
     for store in stores:
         store.wait()
-    for copy in fcopies + every:
-        copy.wait_send()
+    wait_send(fcopies + every)
 
 
 def on_device(

time: 31.8 us -> 29.9 us (0.940)
  the two profiles are of different devices: /device:TPU:0 before, /device:TPU:24 now
where the time goes in v5:
time: 29.9 us; the launch traced here: 29.7 us
  Pallas kernels  27.8 us (93%)
  local copies, waits for them, and re-layouts  1.87 us (6%)
    pallas_call x1, Pallas kernels, on_device(): pl.pallas_call(functools.partial(kernel, nr, nc), out_shape=jax.ShapeDtyp...  27.8 us
    unnamed x1, local copies, waits for them, and re-layouts  1.87 us

profile of v5, /device:TPU:24, one launch (start us, length us, event | category | flops | bytes accessed | tf_op | source)
XLA Modules:
  0.0 29.7 jit_solution(16728103872186038543)
XLA Ops:
  0.0 27.8 %shard_map.118 = bf16[64,32,128]{2,1,0:T(8,128)(2,1)} custom-call(bf16[16,64,180]{2,1,0:T(8,128)(2,1)} %feat.1, f32[180]{0:T(256)} %gain1.1, bf16[180,540]{1,0:T(8,128)(2,1)} %qkv.1, f32[6,1521]{1,0:T(8,128)} %bitcast.7, bf16[180,180]{1,0:T(8,128)(2,1)} %proj.1, f32[180]{0:T(256)} %gain2.1, bf16[180,360]{1,0:T(8,128)(2,1)} %hid.1, bf16[180,360]{1,0:T(8,128)(2,1)} %bitcast.6, ...), custom_call_target="tpu_custom_call" | custom-call | tf_op jit(solution)/shard_map/pallas_call | solution.py:672
  27.8 1.9 %copy.14 = bf16[64,32,128]{2,1,0:T(8,128)(2,1)} copy(bf16[64,32,128]{2,1,0:T(8,128)(2,1)} %shard_map.118) | data formatting | bytes 1048576

commit v6 on v5

--- a/solution.py
+++ b/solution.py
@@ -192,15 +192,19 @@
             for half in range(2)
         ]
 
-    for part in range(2):
+    corner_place = ((4, 8), (4, 64), (16, 8), (16, 64))
+    pl.semaphore_wait(barrier, expected)
+    for part, corners in ((0, (3, 1)), (1, (0, 2))):
+        for corner in corners:
+            first_row, first_col = corner_place[corner]
+            send_c[corner] = pack_pixels(*region(fpad, first_row, 4, first_col, 8))
         send_t[part] = pack_pixels(*region(fpad, 4, 4, 8 + 32 * part, 32))
         send_b[part] = pack_pixels(*region(fpad, 16, 4, 8 + 32 * part, 32))
-    send_l[...] = pack_pixels(*region(fpad, 4, TH, 8, 8))
-    send_r[...] = pack_pixels(*region(fpad, 4, TH, 64, 8))
-    for corner, (first_row, first_col) in enumerate(((4, 8), (4, 64), (16, 8), (16, 64))):
-        send_c[corner] = pack_pixels(*region(fpad, first_row, 4, first_col, 8))
-    pl.semaphore_wait(barrier, expected)
-    start(fcopies)
+        if part == 0:
+            send_r[...] = pack_pixels(*region(fpad, 4, TH, 64, 8))
+        else:
+            send_l[...] = pack_pixels(*region(fpad, 4, TH, 8, 8))
+        start(fcopies[5 * part : 5 * part + 5])
     for name in ("qkv", "proj", "gain2", "hid", "outw", "gconv", "bconv", "uconv"):
         local[name].start()
 
@@ -338,15 +342,18 @@
             axis=0,
         )
 
-    def project_keys(w):
-        keys_in = jnp.concatenate(
-            [pixels(npad, half, w, 0, KWIN, 4, KWIN).astype(BF16) for half in range(2)], axis=1
-        )
-        xwin[...] = keys_in
-        kwin[w] = mm(keys_in, wk[...]).astype(BF16)
+    def project_keys(w, spans):
+        for first, count in spans:
+            keys_in = jnp.concatenate(
+                [pixels(npad, half, w, first, count, 4, KWIN).astype(BF16) for half in range(2)],
+                axis=1,
+            )
+            rows = slice(KWIN * first, KWIN * (first + count))
+            xwin[w, rows, :] = keys_in
+            kwin[w, rows, :] = mm(keys_in, wk[...]).astype(BF16)
 
     def project_values(w):
-        vwin[w] = jnp.where(ones_row, 1.0, mm_nt(wvt[...], xwin[...])).astype(BF16)
+        vwin[w] = jnp.where(ones_row, 1.0, mm_nt(wvt[...], xwin[w])).astype(BF16)
 
     def project_queries(w):
         query_in = jnp.concatenate(
@@ -354,19 +361,27 @@
         )
         qwin[w] = mm_nt(wqt[...], query_in) * QSCALE
 
-    def score(number, w, head):
+    whole_keys = ((0, 288), (288, 576))
+    own_keys = ((96, 288), (288, 480))
+    halo_keys = ((0, 96), (480, 576))
+    inner_from = 2 * HEADS
+
+    def slot(number):
+        return number % 2 if number < inner_from else 2 + number - inner_from
+
+    def score(number, w, head, spans):
         mine = (r >= HEAD * head) & (r < HEAD * (head + 1))
         q = jnp.where(mine, qwin[w], 0.0).astype(BF16)
-        top = None
-        for part in (slice(0, 288), slice(288, 576)):
-            scores = mm(kwin[w, part, :], q) + bias[head, part, :]
-            sbuf[number % 2, part, :] = scores
+        top = tops.get(number)
+        for first, last in spans:
+            scores = mm(kwin[w, first:last, :], q) + bias[head, first:last, :]
+            sbuf[slot(number), first:last, :] = scores
             best = jnp.max(scores, axis=0, keepdims=True)
             top = best if top is None else jnp.maximum(top, best)
         tops[number] = top
 
     def exponent(number):
-        pbuf[number % 2] = jnp.exp2(sbuf[number % 2] - tops[number]).astype(BF16)
+        pbuf[number % 2] = jnp.exp2(sbuf[slot(number)] - tops[number]).astype(BF16)
 
     def combine(number, w, head):
         rows = slice(SLOT * head, SLOT * (head + 1))
@@ -434,7 +449,7 @@
 
     def first_half():
         halo_pixels(0)
-        project_keys(0)
+        project_keys(0, ((0, KWIN),))
         project_values(0)
         attend(0, 3)
 
@@ -450,13 +465,16 @@
         for number in range(begin, end):
             turn, head = divmod(number, HEADS)
             if number < len(steps):
-                score(number, windows[turn], head)
+                inner_window = number >= inner_from
+                score(number, windows[turn], head, halo_keys if inner_window else whole_keys)
             if 0 <= number - 1 < len(steps):
                 exponent(number - 1)
             if 0 <= number - 2:
                 combine(number - 2, *steps[number - 2])
-            if turn + 1 < len(windows) and 3 <= head <= 4:
-                (project_keys, project_values)[head - 3](windows[turn + 1])
+            if turn + 1 < len(windows) and head == 3:
+                project_keys(windows[turn + 1], ((0, 4), (20, 4)) if turn else ((0, KWIN),))
+            if turn + 1 < len(windows) and head == 4:
+                project_values(windows[turn + 1])
             if 0 < turn < len(windows):
                 if head == 1:
                     merge_heads(windows[turn - 1])
@@ -469,7 +487,14 @@
         for w in windows:
             project_queries(w)
 
+    def own_scores():
+        for w in windows[2:]:
+            project_keys(w, ((4, TH),))
+        for number in range(inner_from, len(steps)):
+            score(number, *steps[number], own_keys)
+
     all_queries()
+    own_scores()
     wait_recv(fcopies[k] for k in (0, 1, 2, 3, 4))
     first_half()
     wait_recv(fcopies[k] for k in (5, 6, 7, 8, 9))
@@ -593,19 +618,16 @@
     def out_half(half):
         ostage[half] = obuf[half].reshape(64, 16, 128).astype(BF16)
 
-    def top_rows():
+    def end_rows():
         conv_group(0, 2)
+        conv_group(17, 2)
         conv_group(2, 1)
+        conv_group(19, 1)
         conv_before(0, 3)
+        conv_before(15, 3)
         conv_up(0)
+        conv_up(3)
         out_half(0)
-
-    def bottom_rows():
-        conv_group(17, 2)
-        conv_group(19, 1)
-        conv_before(15, 3)
-        conv_up(3)
-        out_half(1)
 
     ybuf[:, 18 * GP :, :] = jnp.zeros((2, 8, 128), F32)
     wait_recv(every[k] for k in (0, 5))
@@ -615,13 +637,12 @@
         pltpu.make_async_copy(ostage.at[half], out.at[:, 16 * half : 16 * half + 16], osem.at[half])
         for half in range(2)
     ]
-    wait_recv(every[k] for k in (2, 4, 7, 9, 11, 13))
+    wait_recv(every[k] for k in (1, 2, 3, 4, 6, 7, 8, 9, 10, 11, 12, 13))
     top_mixed()
-    top_rows()
+    bottom_mixed()
+    end_rows()
     stores[0].start()
-    wait_recv(every[k] for k in (1, 3, 6, 8, 10, 12))
-    bottom_mixed()
-    bottom_rows()
+    out_half(1)
     stores[1].start()
     for store in stores:
         store.wait()
@@ -659,9 +680,9 @@
         pltpu.VMEM((256, 384), BF16), pltpu.VMEM((256, 384), BF16), pltpu.VMEM((384, 256), BF16),
         pltpu.VMEM((9, 256, 256), BF16), pltpu.VMEM((3, 256, 256), BF16),
         pltpu.VMEM((3, 256, 256), BF16), pltpu.VMEM((3, 256, 256), BF16),
-        pltpu.VMEM((HEADS, KWIN * KWIN, 256), F32), pltpu.VMEM((KWIN * KWIN, 256), BF16),
+        pltpu.VMEM((HEADS, KWIN * KWIN, 256), F32), pltpu.VMEM((4, KWIN * KWIN, 256), BF16),
         pltpu.VMEM((4, KWIN * KWIN, 256), BF16), pltpu.VMEM((4, 192, KWIN * KWIN), BF16),
-        pltpu.VMEM((4, 256, 256), F32), pltpu.VMEM((2, KWIN * KWIN, 256), F32),
+        pltpu.VMEM((4, 256, 256), F32), pltpu.VMEM((14, KWIN * KWIN, 256), F32),
         pltpu.VMEM((2, KWIN * KWIN, 256), BF16), pltpu.VMEM((4, 192, 256), BF16),
         pltpu.VMEM((256, 256), F32), pltpu.VMEM((256, 256), BF16), pltpu.VMEM((256, 384), BF16),
         pltpu.VMEM((2, 64 * 16, 128), F32), pltpu.VMEM((2, 64, 16, 128), BF16),

time: 29.9 us -> 28.1 us (0.940)
  Pallas kernels: 27.8 us -> 26 us
    pallas_call x1, Pallas kernels: 27.8 us -> 26 us  [on_device(): pl.pallas_call(functools.partial(kernel, nr, nc), out_shape=jax.ShapeDtyp...]
where the time goes in v6:
time: 28.1 us; the launch traced here: 27.9 us
  Pallas kernels  26 us (93%)
  local copies, waits for them, and re-layouts  1.87 us (7%)
    pallas_call x1, Pallas kernels, on_device(): pl.pallas_call(functools.partial(kernel, nr, nc), out_shape=jax.ShapeDtyp...  26 us
    unnamed x1, local copies, waits for them, and re-layouts  1.87 us

profile of v6, /device:TPU:24, one launch (start us, length us, event | category | flops | bytes accessed | tf_op | source)
XLA Modules:
  0.0 27.9 jit_solution(14205741564453982003)
XLA Ops:
  0.0 26.0 %shard_map.118 = bf16[64,32,128]{2,1,0:T(8,128)(2,1)} custom-call(bf16[16,64,180]{2,1,0:T(8,128)(2,1)} %feat.1, f32[180]{0:T(256)} %gain1.1, bf16[180,540]{1,0:T(8,128)(2,1)} %qkv.1, f32[6,1521]{1,0:T(8,128)} %bitcast.7, bf16[180,180]{1,0:T(8,128)(2,1)} %proj.1, f32[180]{0:T(256)} %gain2.1, bf16[180,360]{1,0:T(8,128)(2,1)} %hid.1, bf16[180,360]{1,0:T(8,128)(2,1)} %bitcast.6, ...), custom_call_target="tpu_custom_call" | custom-call | tf_op jit(solution)/shard_map/pallas_call | solution.py:693
  26.0 1.9 %copy.14 = bf16[64,32,128]{2,1,0:T(8,128)(2,1)} copy(bf16[64,32,128]{2,1,0:T(8,128)(2,1)} %shard_map.118) | data formatting | bytes 1048576

commit v7 on v6

--- a/solution.py
+++ b/solution.py
@@ -227,22 +227,18 @@
             )
 
     own_pixels()
-    for ref in (qpad, ppad, hpad, opad, gpad, bpad):
+    for ref in (qpad, ppad, hpad, opad):
         ref[...] = jnp.zeros(ref.shape, ref.dtype)
-    for a in range(3):
-        upad[a, 192:256, :] = jnp.zeros((64, 256), BF16)
 
     r = iota((256, 256), 0)
     c = iota((256, 256), 1)
     identity = one_hot(r == c)
 
-    def prepare_bias():
+    def select_bias():
         whole = jnp.concatenate(
             [table_v[...] * LOG2E, jnp.zeros((HEADS, 1536 - TABLE), F32)], axis=1
         )
         whole = jnp.concatenate([whole, jnp.zeros((2, 1536), F32)], axis=0)
-        lane8 = iota((8, 128), 1)
-        sub8 = iota((8, 128), 0)
         pieces = []
         for tile in range(5):
             first = SIDE * (SIDE - 8 - 8 * tile)
@@ -253,37 +249,39 @@
         mid = rest.astype(BF16)
         low = (rest - mid.astype(F32)).astype(BF16)
         picked = mm(hi, sel_v[...]) + mm(mid, sel_v[...]) + mm(low, sel_v[...])
-        lane24 = iota((KWIN, 128), 1)
-        for head in range(HEADS):
-            tiles = []
-            for tile in range(5):
-                z = picked[8 * tile + head : 8 * tile + head + 1, :]
-                blocks = []
-                for part, base in ((1, 7), (0, 15), (0, 7)):
-                    first = jnp.broadcast_to(z[:, 128 * part : 128 * part + 128], (8, 128))
-                    second = jnp.broadcast_to(z[:, 128 * part + 128 : 128 * part + 256], (8, 128))
-                    first = pltpu.roll(first, 128 - base, 1, stride=1, stride_axis=0)
-                    second = pltpu.roll(second, 16 - base, 1, stride=1, stride_axis=0)
-                    blocks.append(jnp.where((lane8 & 15) + base - sub8 < 16, first, second))
-                tiles.append(jnp.concatenate(blocks, axis=0))
-            for shift in range(8):
-                amount = 16 * shift
-                if shift:
-                    rolled = [pltpu.roll(t, 128 - amount, 1) for t in tiles]
-                    joined = [
-                        jnp.where(lane24 < 128 - amount, rolled[k], rolled[k + 1]) for k in range(4)
-                    ]
-                else:
-                    joined = tiles
-                for block in range(3):
-                    p = KWIN - 1 - 8 * block - shift
-                    for half in range(2):
-                        bias[head, KWIN * p : KWIN * (p + 1), 128 * half : 128 * half + 128] = (
-                            joined[block + half]
-                        )
-
-    arrive("table", "selector")
-    prepare_bias()
+        return picked
+
+    lane8 = iota((8, 128), 1)
+    sub8 = iota((8, 128), 0)
+    lane24 = iota((KWIN, 128), 1)
+
+    def head_bias(picked, head):
+        tiles = []
+        for tile in range(5):
+            z = picked[8 * tile + head : 8 * tile + head + 1, :]
+            blocks = []
+            for part, base in ((1, 7), (0, 15), (0, 7)):
+                first = jnp.broadcast_to(z[:, 128 * part : 128 * part + 128], (8, 128))
+                second = jnp.broadcast_to(z[:, 128 * part + 128 : 128 * part + 256], (8, 128))
+                first = pltpu.roll(first, 128 - base, 1, stride=1, stride_axis=0)
+                second = pltpu.roll(second, 16 - base, 1, stride=1, stride_axis=0)
+                blocks.append(jnp.where((lane8 & 15) + base - sub8 < 16, first, second))
+            tiles.append(jnp.concatenate(blocks, axis=0))
+        for shift in range(8):
+            amount = 16 * shift
+            if shift:
+                rolled = [pltpu.roll(t, 128 - amount, 1) for t in tiles]
+                joined = [
+                    jnp.where(lane24 < 128 - amount, rolled[k], rolled[k + 1]) for k in range(4)
+                ]
+            else:
+                joined = tiles
+            for block in range(3):
+                p = KWIN - 1 - 8 * block - shift
+                for half in range(2):
+                    bias[head, KWIN * p : KWIN * (p + 1), 128 * half : 128 * half + 128] = (
+                        joined[block + half]
+                    )
 
     def prepare_weights():
         qpad[0:CH, 0 : 3 * CH] = qkv_v[...]
@@ -291,26 +289,39 @@
         wk[...] = mm(qpad[:, 128:384], one_hot((r == c + 52) & (c < CH))).astype(BF16)
         rv = iota((192, 384), 0)
         cv = iota((192, 384), 1)
-        slot_source = HEAD * lax.shift_right_logical(rv, 5) + (rv & 31)
-        wvt[...] = mm_nt(one_hot((cv == slot_source + 104) & ((rv & 31) < HEAD)), qpad[:, 256:640]).astype(BF16)
+        source = HEAD * lax.shift_right_logical(rv, 5) + (rv & 31)
+        wvt[...] = mm_nt(one_hot((cv == source + 104) & ((rv & 31) < HEAD)), qpad[:, 256:640]).astype(BF16)
+
+    def proj_weights():
         ppad[0:CH, 0:CH] = proj_v[...]
-        slot_source = HEAD * lax.shift_right_logical(r, 5) + (r & 31)
-        pw[...] = mm(one_hot((c == slot_source) & ((r & 31) < HEAD) & (r < 192)), ppad[...]).astype(BF16)
+        source = HEAD * lax.shift_right_logical(r, 5) + (r & 31)
+        pw[...] = mm(one_hot((c == source) & ((r & 31) < HEAD) & (r < 192)), ppad[...]).astype(BF16)
         hpad[0:CH, 0 : 2 * CH] = hid_v[...]
+
+    def out_weights():
         opad[0:CH, 0 : 2 * CH] = outw_v[...]
         wout[...] = mm_nt(one_hot(iota((384, 384), 0) == iota((384, 384), 1)), opad[...]).astype(BF16)
-        for tap in range(9):
-            gpad[tap, 0:CH, 0:CH] = gconv_v[tap // 3, tap % 3]
+
+    def conv_weights(a):
+        for b in range(3):
+            tap = 3 * a + b
+            gpad[tap] = jnp.zeros((256, 256), BF16)
+            gpad[tap, 0:CH, 0:CH] = gconv_v[a, b]
+        bpad[a] = jnp.zeros((256, 256), BF16)
+        upad[a, 192:256, :] = jnp.zeros((64, 256), BF16)
         order = 4 * (r & 63) + 2 * (lax.shift_right_logical(r, 6) & 1) + lax.shift_right_logical(r, 7)
-        shuffle_rows = one_hot(c == order)
-        for a in range(3):
-            for b in range(3):
-                bpad[a, 64 * b : 64 * (b + 1), 0:CH] = bconv_v[a, b]
-            w2[a] = mm_nt(identity, bpad[a]).astype(BF16)
-            w3[a] = mm_nt(shuffle_rows, upad[a]).astype(BF16)
-
-    arrive("qkv", "proj", "gain2", "hid", "outw", "gconv", "bconv", "uconv")
+        for b in range(3):
+            bpad[a, 64 * b : 64 * (b + 1), 0:CH] = bconv_v[a, b]
+        w2[a] = mm_nt(identity, bpad[a]).astype(BF16)
+        w3[a] = mm_nt(one_hot(c == order), upad[a]).astype(BF16)
+
+    late_weights = [
+        proj_weights, out_weights, functools.partial(conv_weights, 0),
+        functools.partial(conv_weights, 1), functools.partial(conv_weights, 2),
+    ]
+    arrive("qkv")
     prepare_weights()
+
     def halo_pixels(part):
         side, rim, has_side = ((halo_l, 0, has_left), (halo_r, 72, has_right))[part]
         groups = [
@@ -328,7 +339,6 @@
                     fpad[half, pl.ds(start, width), :] = x[half][k * width : (k + 1) * width]
             store_normed(x, starts)
 
-    g2 = lanes256(gain2_v)
     inside = c < CH
     ones_row = (iota((192, KWIN * KWIN), 0) & 31) == HEAD
     tops = {}
@@ -471,6 +481,8 @@
                 exponent(number - 1)
             if 0 <= number - 2:
                 combine(number - 2, *steps[number - 2])
+            if number < len(late_weights):
+                late_weights[number]()
             if turn + 1 < len(windows) and head == 3:
                 project_keys(windows[turn + 1], ((0, 4), (20, 4)) if turn else ((0, KWIN),))
             if turn + 1 < len(windows) and head == 4:
@@ -490,11 +502,19 @@
     def own_scores():
         for w in windows[2:]:
             project_keys(w, ((4, TH),))
-        for number in range(inner_from, len(steps)):
-            score(number, *steps[number], own_keys)
+        picked = select_bias()
+        head_bias(picked, 0)
+        for head in range(HEADS):
+            score(inner_from + head, windows[2], head, own_keys)
+            if head + 1 < HEADS:
+                head_bias(picked, head + 1)
+            score(inner_from + HEADS + head, windows[3], head, own_keys)
 
     all_queries()
+    arrive("table", "selector")
     own_scores()
+    arrive("proj", "gain2", "hid", "outw", "gconv", "bconv", "uconv")
+    g2 = lanes256(gain2_v)
     wait_recv(fcopies[k] for k in (0, 1, 2, 3, 4))
     first_half()
     wait_recv(fcopies[k] for k in (5, 6, 7, 8, 9))
@@ -692,7 +712,7 @@
     ]
     result = pl.pallas_call(
         functools.partial(kernel, nr, nc),
-        out_shape=jax.ShapeDtypeStruct((64, 2 * TH, 2 * TW), BF16),
+        out_shape=pltpu.VMEM((64, 2 * TH, 2 * TW), BF16),
         in_specs=[any_space] * len(operands),
         out_specs=pl.BlockSpec(memory_space=pl.ANY),
         scratch_shapes=scratch,

time: 28.1 us -> 26.5 us (0.943)
  local copies, waits for them, and re-layouts: 1.87 us -> 0.8 us
  Pallas kernels: 26 us -> 25.5 us
    unnamed x1, local copies, waits for them, and re-layouts: 1.87 us -> 0.8 us
    pallas_call x1, Pallas kernels: 26 us -> 25.5 us  [on_device(): pl.pallas_call(functools.partial(kernel, nr, nc), out_shape=pltpu.VMEM((6...]
where the time goes in v7:
time: 26.5 us; the launch traced here: 26.3 us
  Pallas kernels  25.5 us (96%)
  local copies, waits for them, and re-layouts  0.8 us (3%)
    pallas_call x1, Pallas kernels, on_device(): pl.pallas_call(functools.partial(kernel, nr, nc), out_shape=pltpu.VMEM((6...  25.5 us
    unnamed x1, local copies, waits for them, and re-layouts  0.8 us

profile of v7, /device:TPU:24, one launch (start us, length us, event | category | flops | bytes accessed | tf_op | source)
XLA Modules:
  0.0 26.3 jit_solution(607417816002108627)
XLA Ops:
  0.0 25.5 %shard_map.118 = bf16[64,32,128]{2,1,0:T(8,128)(2,1)S(1)} custom-call(bf16[16,64,180]{2,1,0:T(8,128)(2,1)} %feat.1, f32[180]{0:T(256)} %gain1.1, bf16[180,540]{1,0:T(8,128)(2,1)} %qkv.1, f32[6,1521]{1,0:T(8,128)} %bitcast.7, bf16[180,180]{1,0:T(8,128)(2,1)} %proj.1, f32[180]{0:T(256)} %gain2.1, bf16[180,360]{1,0:T(8,128)(2,1)} %hid.1, ...), custom_call_target="tpu_custom_call" | custom-call | tf_op jit(solution)/shard_map/pallas_call | solution.py:713
  25.5 0.8 %copy.14 = bf16[64,32,128]{2,1,0:T(8,128)(2,1)} copy(bf16[64,32,128]{2,1,0:T(8,128)(2,1)S(1)} %shard_map.118) | data formatting | bytes 1048576

commit v8 on v7

--- a/solution.py
+++ b/solution.py
@@ -157,16 +157,16 @@
 
     fcopies = exchange(
         [
+            (send_r, halo_l, "r"),
+            (send_t.at[0], halo_b.at[0], "u"),
+            (send_b.at[0], halo_t.at[0], "d"),
             (send_c.at[3], halo_c.at[0], "dr"),
             (send_c.at[1], halo_c.at[2], "ur"),
-            (send_t.at[0], halo_b.at[0], "u"),
-            (send_b.at[0], halo_t.at[0], "d"),
-            (send_r, halo_l, "r"),
-            (send_c.at[0], halo_c.at[3], "ul"),
-            (send_c.at[2], halo_c.at[1], "dl"),
             (send_l, halo_r, "l"),
             (send_t.at[1], halo_b.at[1], "u"),
             (send_b.at[1], halo_t.at[1], "d"),
+            (send_c.at[0], halo_c.at[3], "ul"),
+            (send_c.at[2], halo_c.at[1], "dl"),
         ],
         fsend, frecv,
     )
@@ -195,16 +195,17 @@
     corner_place = ((4, 8), (4, 64), (16, 8), (16, 64))
     pl.semaphore_wait(barrier, expected)
     for part, corners in ((0, (3, 1)), (1, (0, 2))):
-        for corner in corners:
-            first_row, first_col = corner_place[corner]
-            send_c[corner] = pack_pixels(*region(fpad, first_row, 4, first_col, 8))
-        send_t[part] = pack_pixels(*region(fpad, 4, 4, 8 + 32 * part, 32))
-        send_b[part] = pack_pixels(*region(fpad, 16, 4, 8 + 32 * part, 32))
         if part == 0:
             send_r[...] = pack_pixels(*region(fpad, 4, TH, 64, 8))
         else:
             send_l[...] = pack_pixels(*region(fpad, 4, TH, 8, 8))
-        start(fcopies[5 * part : 5 * part + 5])
+        send_t[part] = pack_pixels(*region(fpad, 4, 4, 8 + 32 * part, 32))
+        send_b[part] = pack_pixels(*region(fpad, 16, 4, 8 + 32 * part, 32))
+        start(fcopies[5 * part : 5 * part + 3])
+        for corner in corners:
+            first_row, first_col = corner_place[corner]
+            send_c[corner] = pack_pixels(*region(fpad, first_row, 4, first_col, 8))
+        start(fcopies[5 * part + 3 : 5 * part + 5])
     for name in ("qkv", "proj", "gain2", "hid", "outw", "gconv", "bconv", "uconv"):
         local[name].start()
 
@@ -628,9 +629,11 @@
                     ]
 
     def inner_rows():
-        for h0 in range(3, 17, 2):
+        for h0 in (3, 5, 7, 9):
             conv_group(h0, 2)
         conv_before(3, 6)
+        for h0 in (11, 13, 15):
+            conv_group(h0, 2)
         conv_before(9, 6)
         conv_up(1)
         conv_up(2)
@@ -640,10 +643,10 @@
 
     def end_rows():
         conv_group(0, 2)
+        conv_group(2, 1)
         conv_group(17, 2)
-        conv_group(2, 1)
+        conv_before(0, 3)
         conv_group(19, 1)
-        conv_before(0, 3)
         conv_before(15, 3)
         conv_up(0)
         conv_up(3)

time: 26.5 us -> 26.4 us (level)
  no operation moved by 1% of the time
where the time goes in v8:
time: 26.4 us; the launch traced here: 26.3 us
  Pallas kernels  25.5 us (97%)
  local copies, waits for them, and re-layouts  0.8 us (3%)
    pallas_call x1, Pallas kernels, on_device(): pl.pallas_call(functools.partial(kernel, nr, nc), out_shape=pltpu.VMEM((6...  25.5 us
    unnamed x1, local copies, waits for them, and re-layouts  0.8 us

profile of v8, /device:TPU:24, one launch (start us, length us, event | category | flops | bytes accessed | tf_op | source)
XLA Modules:
  0.0 26.3 jit_solution(14480584410128342050)
XLA Ops:
  0.0 25.5 %shard_map.118 = bf16[64,32,128]{2,1,0:T(8,128)(2,1)S(1)} custom-call(bf16[16,64,180]{2,1,0:T(8,128)(2,1)} %feat.1, f32[180]{0:T(256)} %gain1.1, bf16[180,540]{1,0:T(8,128)(2,1)} %qkv.1, f32[6,1521]{1,0:T(8,128)} %bitcast.7, bf16[180,180]{1,0:T(8,128)(2,1)} %proj.1, f32[180]{0:T(256)} %gain2.1, bf16[180,360]{1,0:T(8,128)(2,1)} %hid.1, ...), custom_call_target="tpu_custom_call" | custom-call | tf_op jit(solution)/shard_map/pallas_call | solution.py:716
  25.5 0.8 %copy.14 = bf16[64,32,128]{2,1,0:T(8,128)(2,1)} copy(bf16[64,32,128]{2,1,0:T(8,128)(2,1)S(1)} %shard_map.118) | data formatting | bytes 1048576

commit v9 on v8

--- a/solution.py
+++ b/solution.py
@@ -482,8 +482,6 @@
                 exponent(number - 1)
             if 0 <= number - 2:
                 combine(number - 2, *steps[number - 2])
-            if number < len(late_weights):
-                late_weights[number]()
             if turn + 1 < len(windows) and head == 3:
                 project_keys(windows[turn + 1], ((0, 4), (20, 4)) if turn else ((0, KWIN),))
             if turn + 1 < len(windows) and head == 4:
@@ -516,6 +514,8 @@
     own_scores()
     arrive("proj", "gain2", "hid", "outw", "gconv", "bconv", "uconv")
     g2 = lanes256(gain2_v)
+    for prepare in late_weights:
+        prepare()
     wait_recv(fcopies[k] for k in (0, 1, 2, 3, 4))
     first_half()
     wait_recv(fcopies[k] for k in (5, 6, 7, 8, 9))

time: 26.4 us -> 26.1 us (0.989)
  Pallas kernels: 25.5 us -> 25.2 us
    pallas_call x1, Pallas kernels: 25.5 us -> 25.2 us  [on_device(): pl.pallas_call(functools.partial(kernel, nr, nc), out_shape=pltpu.VMEM((6...]
where the time goes in v9:
time: 26.1 us; the launch traced here: 26 us
  Pallas kernels  25.2 us (97%)
  local copies, waits for them, and re-layouts  0.8 us (3%)
    pallas_call x1, Pallas kernels, on_device(): pl.pallas_call(functools.partial(kernel, nr, nc), out_shape=pltpu.VMEM((6...  25.2 us
    unnamed x1, local copies, waits for them, and re-layouts  0.8 us

profile of v9, /device:TPU:24, one launch (start us, length us, event | category | flops | bytes accessed | tf_op | source)
XLA Modules:
  0.0 26.0 jit_solution(149505831267073360)
XLA Ops:
  0.0 25.2 %shard_map.118 = bf16[64,32,128]{2,1,0:T(8,128)(2,1)S(1)} custom-call(bf16[16,64,180]{2,1,0:T(8,128)(2,1)} %feat.1, f32[180]{0:T(256)} %gain1.1, bf16[180,540]{1,0:T(8,128)(2,1)} %qkv.1, f32[6,1521]{1,0:T(8,128)} %bitcast.7, bf16[180,180]{1,0:T(8,128)(2,1)} %proj.1, f32[180]{0:T(256)} %gain2.1, bf16[180,360]{1,0:T(8,128)(2,1)} %hid.1, ...), custom_call_target="tpu_custom_call" | custom-call | tf_op jit(solution)/shard_map/pallas_call | solution.py:716
  25.2 0.8 %copy.14 = bf16[64,32,128]{2,1,0:T(8,128)(2,1)} copy(bf16[64,32,128]{2,1,0:T(8,128)(2,1)S(1)} %shard_map.118) | data formatting | bytes 1048576

commit v10 on v9

--- a/solution.py
+++ b/solution.py
@@ -157,14 +157,14 @@
 
     fcopies = exchange(
         [
+            (send_b.at[0], halo_t.at[0], "d"),
             (send_r, halo_l, "r"),
             (send_t.at[0], halo_b.at[0], "u"),
-            (send_b.at[0], halo_t.at[0], "d"),
             (send_c.at[3], halo_c.at[0], "dr"),
             (send_c.at[1], halo_c.at[2], "ur"),
+            (send_b.at[1], halo_t.at[1], "d"),
             (send_l, halo_r, "l"),
             (send_t.at[1], halo_b.at[1], "u"),
-            (send_b.at[1], halo_t.at[1], "d"),
             (send_c.at[0], halo_c.at[3], "ul"),
             (send_c.at[2], halo_c.at[1], "dl"),
         ],
@@ -195,13 +195,14 @@
     corner_place = ((4, 8), (4, 64), (16, 8), (16, 64))
     pl.semaphore_wait(barrier, expected)
     for part, corners in ((0, (3, 1)), (1, (0, 2))):
+        send_b[part] = pack_pixels(*region(fpad, 16, 4, 8 + 32 * part, 32))
+        start(fcopies[5 * part : 5 * part + 1])
         if part == 0:
             send_r[...] = pack_pixels(*region(fpad, 4, TH, 64, 8))
         else:
             send_l[...] = pack_pixels(*region(fpad, 4, TH, 8, 8))
         send_t[part] = pack_pixels(*region(fpad, 4, 4, 8 + 32 * part, 32))
-        send_b[part] = pack_pixels(*region(fpad, 16, 4, 8 + 32 * part, 32))
-        start(fcopies[5 * part : 5 * part + 3])
+        start(fcopies[5 * part + 1 : 5 * part + 3])
         for corner in corners:
             first_row, first_col = corner_place[corner]
             send_c[corner] = pack_pixels(*region(fpad, first_row, 4, first_col, 8))
@@ -430,7 +431,7 @@
             mix_sr[...] = pack_pixels(*region(mixpad, 3, TH, 64, 8))
             mix_sc[1] = pack_pixels(*region(mixpad, 3, 4, 64, 8))
             mix_sc[3] = pack_pixels(*region(mixpad, 15, 4, 64, 8))
-        start(mcopies[w])
+        start(mcopies[w] if w in (0, 3) else mcopies[w][::-1])
 
     def strip(w):
         cols = slice(w * WIN, (w + 1) * WIN)

time: 26.1 us -> 26.4 us (1.011)
  Pallas kernels: 25.2 us -> 25.5 us
    pallas_call x1, Pallas kernels: 25.2 us -> 25.5 us  [on_device(): pl.pallas_call(functools.partial(kernel, nr, nc), out_shape=pltpu.VMEM((6...]
where the time goes in v10:
time: 26.4 us; the launch traced here: 26.3 us
  Pallas kernels  25.5 us (97%)
  local copies, waits for them, and re-layouts  0.8 us (3%)
    pallas_call x1, Pallas kernels, on_device(): pl.pallas_call(functools.partial(kernel, nr, nc), out_shape=pltpu.VMEM((6...  25.5 us
    unnamed x1, local copies, waits for them, and re-layouts  0.8 us

profile of v10, /device:TPU:24, one launch (start us, length us, event | category | flops | bytes accessed | tf_op | source)
XLA Modules:
  0.0 26.3 jit_solution(14174698646276557034)
XLA Ops:
  0.0 25.5 %shard_map.118 = bf16[64,32,128]{2,1,0:T(8,128)(2,1)S(1)} custom-call(bf16[16,64,180]{2,1,0:T(8,128)(2,1)} %feat.1, f32[180]{0:T(256)} %gain1.1, bf16[180,540]{1,0:T(8,128)(2,1)} %qkv.1, f32[6,1521]{1,0:T(8,128)} %bitcast.7, bf16[180,180]{1,0:T(8,128)(2,1)} %proj.1, f32[180]{0:T(256)} %gain2.1, bf16[180,360]{1,0:T(8,128)(2,1)} %hid.1, ...), custom_call_target="tpu_custom_call" | custom-call | tf_op jit(solution)/shard_map/pallas_call | solution.py:717
  25.5 0.8 %copy.14 = bf16[64,32,128]{2,1,0:T(8,128)(2,1)} copy(bf16[64,32,128]{2,1,0:T(8,128)(2,1)S(1)} %shard_map.118) | data formatting | bytes 1048576
